TPU v7x, 768 devices: a whole 4x8x12 slice. The times are simulated.
768 devices in a mesh: feat: 16 (over x_hi, y), batch: 24 (over x_lo, z), twin: 2 (over core).
Axes of the slice: x: 4 (x_hi: 2, x_lo: 2; x = x_hi * 2 + x_lo), y: 8, z: 12, core: 2. Of those that a mesh axis runs over, the one named last changes fastest.
Arguments:
- hidden_act: bfloat16 [2, 3072, 8192], P('twin', 'batch'), as said below
- proj_weight: bfloat16 [8192, 4608], P(None, 'feat'), may hold values from -0.0625 to 0.0625
Outputs:
- grad_normed: float32 [4608, 2, 3072], P(('feat', 'twin'), None, 'batch')
Inputs may be any that keep to these rules, and one draw needn't show every extreme that they name: `hidden_act`: row r of both views is the same sample.
All inputs are finite; a program needn't handle non-finite values.
Results may differ from a plain program's by a relative error of at most 0.012.
The roundings to bfloat16 on the way count: a program that leaves them out, or rounds other values in their place, can miss the bound.
Values may be sent and summed in bfloat16 or wider, within the bound.
No kernel may reach another device: no remote copies, remote signals or barrier semaphores. Data moves between devices by JAX's collectives and lax.ppermute only.
A program may use at most 64 MiB of HBM per device.

v0:
```python
import jax
import jax.numpy as jnp
from jax import lax
from jax.sharding import PartitionSpec as P

epsilon = 1e-05
off_weight = 0.0051


def shards(hidden_act, proj_weight):
    view_rows = hidden_act[0]
    rows_here = view_rows.shape[0]
    row_total = rows_here * lax.axis_size("batch")
    projected = lax.dot_general(
        proj_weight, view_rows, (((0,), (1,)), ((), ())), preferred_element_type=jnp.float32
    )
    row_sums, squares = lax.psum(
        (jnp.sum(projected, axis=1), jnp.sum(projected * projected, axis=1)), "batch"
    )
    feat_mean = row_sums / row_total
    feat_var = squares / row_total - feat_mean * feat_mean
    normed = ((projected - feat_mean[:, None]) * lax.rsqrt(feat_var + epsilon)[:, None]).astype(
        jnp.bfloat16
    )
    gathered = lax.all_gather(normed, ("feat", "twin"), axis=0, tiled=True)
    groups = lax.axis_size(("feat", "twin"))
    feat_here = normed.shape[0]
    block_size = feat_here // 2
    paired = gathered.reshape(groups // 2, 2, feat_here, rows_here)
    first_view = paired[:, 0].reshape(groups, block_size, rows_here)
    second_view = paired[:, 1].reshape(groups, block_size, rows_here)
    first_twice = jnp.concatenate([first_view, first_view], axis=0)
    second_twice = jnp.concatenate([second_view, second_view], axis=0)
    band_index = lax.axis_index(("feat", "twin"))
    second_turned = lax.dynamic_slice_in_dim(second_twice, band_index, groups, 0)
    share_rows = block_size // lax.axis_size("batch")
    shares = lax.psum_scatter(
        jnp.einsum("kir,kjr->ikj", first_view, second_turned, preferred_element_type=jnp.float32),
        "batch",
        scatter_dimension=0,
        tiled=True,
    )
    corr_block = shares / row_total
    row_ids = (
        lax.broadcasted_iota(jnp.int32, corr_block.shape, 0) + lax.axis_index("batch") * share_rows
    )
    col_ids = lax.broadcasted_iota(jnp.int32, corr_block.shape, 2)
    diagonal = (band_index == 0) & (row_ids == col_ids)
    grad_part = jnp.where(
        diagonal, -2.0 * (1.0 - corr_block), 2.0 * off_weight * corr_block
    ).astype(jnp.bfloat16)
    grad_band = lax.all_gather(grad_part, "batch", axis=0, tiled=True)
    grad_twice = jnp.concatenate([grad_band, grad_band], axis=1)
    first_block = jnp.int32(0) // block_size
    blocks = block_size * lax.axis_size(("feat", "twin")) // block_size
    second_fwd = lax.dynamic_slice_in_dim(second_twice, band_index, blocks, 0)
    out_first = jnp.einsum(
        "ikj,kjr->kir", grad_band, second_fwd, preferred_element_type=jnp.float32
    )
    back_start = first_block - band_index + groups
    grad_back = lax.dynamic_slice_in_dim(grad_twice, back_start, blocks, 1)
    first_back = lax.dynamic_slice_in_dim(first_twice, back_start, blocks, 0)
    out_second = jnp.einsum(
        "ikj,kir->kjr", grad_back, first_back, preferred_element_type=jnp.float32
    )
    return lax.psum_scatter(
        jnp.stack([out_first, out_second], axis=2).reshape(
            block_size * lax.axis_size(("feat", "twin")), 2, rows_here
        ),
        ("feat", "twin"),
        scatter_dimension=0,
        tiled=True,
    )


def solution(mesh):
    return jax.shard_map(
        shards,
        mesh=mesh,
        in_specs=(P("twin", "batch", None), P(None, "feat")),
        out_specs=P(("feat", "twin"), None, "batch"),
        check_vma=False,
    )
```

profile of v0, /device:TPU:1, one launch (start us, length us, event | category | flops | bytes accessed | tf_op | source)
XLA Modules:
  0.0 696.6 jit_solution(16191857822429233331)
XLA Ops:
  6.5 1.6 copy-done
  8.1 3.9 fusion.14
  12.0 49.2 %all-reduce.1 = (f32[288]{0:T(512)S(1)}, f32[288]{0:T(512)S(1)}) all-reduce(f32[288]{0:T(512)S(1)} %get-tuple-element.6, f32[288]{0:T(512)S(1)} %get-tuple-element.5), channel_id=1, replica_groups=mesh['feat'=16,'batch'=24,'twin'=2] {'batch'}, use_global_device_ids=true, to_apply=%region_3.0 | all-reduce | flops 576 | bytes 4608 | tf_op jit(solution)/shard_map/psum | solution.py:17
  61.2 0.8 multiply_convert_fusion
  62.0 0.0 reduce-scatter.2.cloned.1.call-start
  62.1 95.8 %all-gather.3.cloned.1.call-done = bf16[9216,128]{1,0:T(8,128)(2,1)} async-done(((bf16[288,128]{1,0:T(8,128)(2,1)}), bf16[9216,128]{1,0:T(8,128)(2,1)}) %all-gather.3.cloned.1.call-update) | async-done | bytes 2359312 | tf_op jit(solution)/shard_map/all_gather | solution.py:25
  157.9 1.8 fusion.15
  159.7 1.0 copy-done.2
  160.7 2.9 convolution_bitcast_fusion
  163.7 6.2 copy.6
  169.9 0.0 reduce-scatter.2.cloned.1.call-update
  169.9 0.0 all-gather.5.cloned.1.call-start
  170.0 99.6 %reduce-scatter.2.cloned.1.call-done = f32[6,32,144]{2,1,0:T(8,128)} async-done(((f32[144,32,144]{2,1,0:T(8,128)}), f32[6,32,144]{2,1,0:T(8,128)}) %reduce-scatter.2.cloned.1.call-update) | async-done | bytes 110608 | tf_op jit(solution)/shard_map/reduce_scatter | solution.py:37
  269.6 1.7 select_convert_fusion
  271.2 0.0 all-gather.5.cloned.1.call-update
  271.2 0.0 all-reduce.4.cloned.1.call-start
  271.3 101.2 %all-gather.5.cloned.1.call-done = bf16[144,32,144]{2,1,0:T(8,128)(2,1)} async-done(((bf16[6,32,144]{2,1,0:T(8,128)(2,1)}), bf16[144,32,144]{2,1,0:T(8,128)(2,1)}) %all-gather.5.cloned.1.call-update) | async-done | bytes 1327120 | tf_op jit(solution)/shard_map/all_gather | solution.py:52
  372.5 4.7 copy.8
  377.2 3.1 fusion.12
  380.3 1.8 fusion.1
  382.1 5.5 pad_maximum_fusion
  387.7 1.3 dynamic-slice
  389.6 298.8 %all-reduce.4.cloned.1.call-done = f32[4608,2,128]{2,1,0:T(2,128)} async-done(((f32[4608,2,128]{2,1,0:T(2,128)}), f32[4608,2,128]{2,1,0:T(2,128)}) %all-reduce.4.cloned.1.call-update) | async-done | bytes 4718608
  688.4 1.6 constant_dynamic-slice_fusion
  (11 shorter events, 0.1 us)
Async XLA Ops:
  6.5 1.6 copy-start
  6.5 151.4 %all-gather.3.cloned.1.call-start = ((), (), s32[]{:S(2)}) async-start(), calls=%async_computation.1 | async-start | bytes 2433024 | tf_op jit(solution)/shard_map/all_gather | solution.py:25
  62.0 207.5 %reduce-scatter.2.cloned.1.call-start = ((), (), s32[]{:S(2)}) async-start(), calls=%async_computation.2 | async-start | bytes 4915200 | tf_op jit(solution)/shard_map/reduce_scatter | solution.py:37
  159.7 1.0 copy-start.2
  169.9 202.6 %all-gather.5.cloned.1.call-start = ((), (), s32[]{:S(2)}) async-start(), calls=%async_computation.3 | async-start | bytes 2457600 | tf_op jit(solution)/shard_map/all_gather | solution.py:52
  271.2 417.2 %all-reduce.4.cloned.1.call-start = ((), (), s32[]{:S(2)}) async-start(), calls=%async_computation.4 | async-start | bytes 9437184
  377.2 3.1 copy-start.1
  377.2 3.1 copy-start.3
Sparse Core Ops, SparseCore 0:
  62.1 95.7 all-gather.2
  170.0 99.4 reduce-scatter.1
  272.0 100.4 all-gather.4
  387.8 300.5 all-reduce.3
where the time goes:
time: 697 us
  waiting for transfers between devices  595 us (85%)
  blocking collectives  49.2 us (7%)
  local copies, waits for them, and re-layouts  18.2 us (3%)
  between operations  13.9 us (2%)
  matrix products  11.7 us (2%)
  other arithmetic  7.98 us (1%)
    unnamed x5, waiting for transfers between devices  299 us
    all_gather x1, waiting for transfers between devices, shards(): grad_band = lax.all_gather(grad_part, 'batch', axis=0, tiled=True)  101 us
    reduce_scatter x1, waiting for transfers between devices, shards(): lax.psum_scatter(jnp.einsum('kir,kjr->ikj', first_view, second_turned, pr...  99.6 us
    all_gather x1, waiting for transfers between devices, shards(): gathered = lax.all_gather(normed, ('feat', 'twin'), axis=0, tiled=True)  95.8 us
    psum x1, blocking collectives, shards(): lax.psum((jnp.sum(projected, axis=1), jnp.sum(projected * projected, axis...  49.2 us
  transfers between devices with their start and end apart: 4, of which 4 were waited for; matrix products, arithmetic and copies ran while one was open for 0% of the time, Pallas kernels for 0%

commit v1 on v0

v1 whole, which is shorter than its diff:
```python
import jax
import jax.numpy as jnp
from jax import lax
from jax.sharding import Mesh
from jax.sharding import PartitionSpec as P

epsilon = 1e-05
off_weight = 0.0051
batch_axes = ("x_lo", "z")
feat_axes = ("x_hi", "y")
bf16, f32 = jnp.bfloat16, jnp.float32


def spread(part, axes):
    copies = jnp.broadcast_to(part[None], (lax.axis_size(axes),) + part.shape)
    return lax.all_to_all(copies, axes, 0, 0, tiled=True)


def shards(hidden_act, proj_weight):
    batches, feats = lax.axis_size(batch_axes), lax.axis_size(feat_axes)
    view_rows = hidden_act[0]
    rows_here = view_rows.shape[0]
    row_total = rows_here * batches
    feat_here = proj_weight.shape[1]
    own = feat_here // batches
    batch_index, feat_index = lax.axis_index(batch_axes), lax.axis_index(feat_axes)
    twin = lax.axis_index("twin")
    projected = lax.dot_general(
        proj_weight, view_rows, (((0,), (1,)), ((), ())), preferred_element_type=f32
    )
    projected = lax.optimization_barrier(projected)
    by_rows = lax.all_to_all(
        projected.reshape(batches, own, rows_here), batch_axes, 0, 0, tiled=True
    )
    feat_mean = jnp.sum(by_rows, axis=(0, 2), keepdims=True) / row_total
    squares = jnp.sum(by_rows * by_rows, axis=(0, 2), keepdims=True) / row_total
    feat_var = squares - feat_mean * feat_mean
    normed = ((by_rows - feat_mean) * lax.rsqrt(feat_var + epsilon)).astype(bf16)
    normed = normed.transpose(1, 0, 2).reshape(own, row_total)
    other = lax.ppermute(normed, "twin", [(0, 1), (1, 0)])
    both = lax.ppermute(normed, "x_lo", [(0, 1), (1, 0)])
    low = lax.axis_index("x_lo") == 0
    pair = jnp.stack([jnp.where(low, normed, both), jnp.where(low, both, normed)])
    here = lax.all_gather(pair, "z", axis=1)
    there = spread(other, feat_axes)
    here = here.reshape(batches * own, row_total)
    there = there.reshape(feats * own, row_total)
    corr = lax.dot_general(
        here, there, (((1,), (1,)), ((), ())), preferred_element_type=f32
    ) / row_total
    row_ids = lax.broadcasted_iota(jnp.int32, corr.shape, 0) + feat_index * feat_here
    cols = lax.broadcasted_iota(jnp.int32, corr.shape, 1)
    col_ids = (cols // own) * feat_here + batch_index * own + cols % own
    grad = jnp.where(
        row_ids == col_ids, -2.0 * (1.0 - corr), 2.0 * off_weight * corr
    ).astype(bf16)
    part = jnp.einsum(
        "ij,jbr->bir",
        grad,
        there.reshape(feats * own, batches, rows_here),
        preferred_element_type=f32,
    ).astype(bf16)
    terms = lax.all_to_all(part, batch_axes, 0, 0, tiled=True)
    total = jnp.sum(terms.astype(f32), axis=0)
    first, second = jnp.split(total, 2, axis=0)
    keep = jnp.where(twin == 0, first, second)
    give = jnp.where(twin == 0, second, first)
    take = lax.ppermute(give, "twin", [(0, 1), (1, 0)])
    return jnp.stack(
        [jnp.where(twin == 0, keep, take), jnp.where(twin == 0, take, keep)], axis=1
    )


def solution(mesh):
    x_parts = 2
    shape = mesh.devices.shape
    fine = Mesh(
        mesh.devices.reshape(
            x_parts, shape[0] // x_parts, x_parts, shape[1] // x_parts, shape[2]
        ),
        ("x_hi", "y", "x_lo", "z", "twin"),
    )
    return jax.shard_map(
        shards,
        mesh=fine,
        in_specs=(P("twin", batch_axes, None), P(None, feat_axes)),
        out_specs=P(feat_axes + ("twin",), None, batch_axes),
        check_vma=False,
    )
```

time: 697 us -> 195 us (0.28)
  waiting for transfers between devices: 595 us -> 102 us
  starting transfers between devices: 0.13 us -> 26.7 us
  blocking collectives: 49.2 us -> 28.7 us
    unnamed x5 -> x1, waiting for transfers between devices: 299 us -> 0.02 us
    all_gather x2 -> x1, waiting for transfers between devices: 197 us -> 0.01 us  [shards(): here = lax.all_gather(pair, 'z', axis=1)]
    reduce_scatter x1 -> x0, waiting for transfers between devices: 99.6 us -> none  [shards(): lax.psum_scatter(jnp.einsum('kir,kjr->ikj', first_view, second_turned, pr...]
    all_to_all x0 -> x2, waiting for transfers between devices: none -> 97.4 us  [the longest x1 59.3 us: shards(): terms = lax.all_to_all(part, batch_axes, 0, 0, tiled=True)]
    psum x1 -> x0, blocking collectives: 49.2 us -> none  [shards(): lax.psum((jnp.sum(projected, axis=1), jnp.sum(projected * projected, axis...]
    all_to_all x0 -> x1, blocking collectives: none -> 28.7 us  [shards(): lax.all_to_all(projected.reshape(batches, own, rows_here), batch_axes, 0,...]
    all_to_all x0 -> x2, starting transfers between devices: none -> 13.9 us  [the longest x1 9.14 us: spread(): return lax.all_to_all(copies, axes, 0, 0, tiled=True)]
    ppermute x0 -> x3, starting transfers between devices: none -> 12.8 us  [the longest x1 6.29 us: shards(): other = lax.ppermute(normed, 'twin', [(0, 1), (1, 0)])]
  transfers between devices with their start and end apart: 4 -> 6, of which waited for: 4 -> 5; matrix products, arithmetic and copies ran while one was open for 0% -> 3% of each run, Pallas kernels for 0% -> 0%
where the time goes in v1:
time: 195 us
  waiting for transfers between devices  102 us (52%)
  blocking collectives  28.7 us (15%)
  starting transfers between devices  26.7 us (14%)
  between operations  13.6 us (7%)
  local copies, waits for them, and re-layouts  11.8 us (6%)
  matrix products  8.79 us (5%)
  other arithmetic  2.88 us (1%)
    all_to_all x1, waiting for transfers between devices, shards(): terms = lax.all_to_all(part, batch_axes, 0, 0, tiled=True)  59.3 us
    all_to_all x1, waiting for transfers between devices, spread(): return lax.all_to_all(copies, axes, 0, 0, tiled=True)  38.1 us
    all_to_all x1, blocking collectives, shards(): lax.all_to_all(projected.reshape(batches, own, rows_here), batch_axes, 0,...  28.7 us
    all_to_all x1, starting transfers between devices, spread(): return lax.all_to_all(copies, axes, 0, 0, tiled=True)  9.14 us
    ppermute x1, starting transfers between devices, shards(): other = lax.ppermute(normed, 'twin', [(0, 1), (1, 0)])  6.29 us
    dot_general x1, matrix products, shards(): jnp.einsum('ij,jbr->bir', grad, there.reshape(feats * own, batches, rows_...  5.08 us
    all_to_all x1, starting transfers between devices, shards(): terms = lax.all_to_all(part, batch_axes, 0, 0, tiled=True)  4.74 us
    ppermute x1, starting transfers between devices, shards(): take = lax.ppermute(give, 'twin', [(0, 1), (1, 0)])  4.38 us
  transfers between devices with their start and end apart: 6, of which 5 were waited for; matrix products, arithmetic and copies ran while one was open for 3% of the time, Pallas kernels for 0%

profile of v1, /device:TPU:1, one launch (start us, length us, event | category | flops | bytes accessed | tf_op | source)
XLA Modules:
  0.0 194.8 jit_solution(2765548198555549283)
XLA Ops:
  6.5 1.6 copy-done
  8.1 3.7 %fusion = f32[288,128]{1,0:T(8,128)S(1)} fusion(bf16[8192,288]{0,1:T(8,128)(2,1)} %param.3, bf16[1,128,8192]{2,1,0:T(8,128)(2,1)S(1)} %copy-done), kind=kOutput, calls=%fused_computation.1 | convolution fusion | flops 603979776 | bytes 6963200 | tf_op jit(solution)/shard_map/dot_general | solution.py:28
  11.9 28.7 %all_to_all.15 = f32[24,12,128]{2,1,0:T(8,128)S(1)} all-to-all(f32[24,12,128]{2,1,0:T(8,128)S(1)} %reshape.31), channel_id=1, replica_groups=mesh['x_hi'=2,'y'=8,'x_lo'=2,'z'=12,'twin'=2] {'x_lo','z'}, dimensions={0} | all-to-all | bytes 294912 | tf_op jit(solution)/shard_map/all_to_all | solution.py:32
  40.6 0.1 fusion.24
  40.7 0.1 fusion.16
  40.9 2.1 %collective-permute-start.1 = (bf16[12,3072]{1,0:T(8,128)(2,1)S(1)}, bf16[12,3072]{1,0:T(8,128)(2,1)S(1)}, u32[]{:S(2)}, u32[]{:S(2)}) collective-permute-start(bf16[12,3072]{1,0:T(8,128)(2,1)S(1)} %bitcast.26), channel_id=1, source_target_pairs={{0,24},{24,0},{1,25},{25,1},{2,26},{26,2},{3,27},{27,3},{4,28},{28... | collective-permute-start | bytes 221192 | tf_op jit(solution)/shard_map/ppermute | solution.py:41
  43.0 3.2 %collective-permute-done.1 = bf16[12,3072]{1,0:T(8,128)(2,1)S(1)} collective-permute-done((bf16[12,3072]{1,0:T(8,128)(2,1)S(1)}, bf16[12,3072]{1,0:T(8,128)(2,1)S(1)}, u32[]{:S(2)}, u32[]{:S(2)}) %collective-permute-start.1) | collective-permute-done | bytes 73760 | tf_op jit(solution)/shard_map/ppermute | solution.py:41
  46.3 0.8 copy.12
  47.1 0.0 all-gather.3.cloned.1.call-update
  47.2 6.3 %collective-permute-start = (bf16[12,3072]{1,0:T(8,128)(2,1)S(1)}, bf16[12,3072]{1,0:T(8,128)(2,1)S(1)}, u32[]{:S(2)}, u32[]{:S(2)}) collective-permute-start(bf16[12,3072]{1,0:T(8,128)(2,1)S(1)} %bitcast.28), channel_id=1, source_target_pairs={{0,1},{1,0},{2,3},{3,2},{4,5},{5,4},{6,7},{7,6},{8,9},{9,8},{10,11... | collective-permute-start | bytes 221192 | tf_op jit(solution)/shard_map/ppermute | solution.py:40
  53.5 0.9 collective-permute-done
  54.4 1.3 broadcast_in_dim.2
  55.7 9.1 %all-to-all-start.1 = ((bf16[16,12,3072]{2,1,0:T(8,128)(2,1)}), bf16[16,12,3072]{2,1,0:T(8,128)(2,1)}, u32[]{:S(2)}, u32[]{:S(2)}) async-start(bf16[16,12,3072]{2,1,0:T(8,128)(2,1)} %broadcast_in_dim.2), calls=%async_computation.1 | async-start | bytes 3145728 | tf_op jit(solution)/shard_map/all_to_all | solution.py:16
  64.9 38.1 %all-to-all-done.1 = bf16[16,12,3072]{2,1,0:T(8,128)(2,1)} async-done(((bf16[16,12,3072]{2,1,0:T(8,128)(2,1)}), bf16[16,12,3072]{2,1,0:T(8,128)(2,1)}, u32[]{:S(2)}, u32[]{:S(2)}) %all-to-all-start.1) | async-done | bytes 1179680 | tf_op jit(solution)/shard_map/all_to_all | solution.py:16
  103.1 1.5 reshape.34
  104.6 3.4 %reshape_reshape.3 = bf16[192,24,128]{2,1,0:T(8,128)(2,1)} reshape(bf16[16,12,3072]{2,1,0:T(8,128)(2,1)} %all-to-all-done.1) | data formatting | bytes 2359296 | tf_op jit(solution)/shard_map/reshape;reshape | solution.py:60
  108.0 3.1 %copy.13 = bf16[2,144,3072]{2,1,0:T(8,128)(2,1)} copy(bf16[2,144,3072]{2,0,1:T(2,128)(2,1)} %all-gather.3.cloned.1.call-done) | data formatting | bytes 3538944 | tf_op jit(solution)/shard_map/all_gather | solution.py:44
  111.1 5.1 %convert_bitcast_fusion = bf16[24,288,128]{2,1,0:T(8,128)(2,1)} fusion(bf16[192,24,128]{2,1,0:T(8,128)(2,1)} %reshape_reshape.3, s32[192]{0:T(256)S(1)} %get-tuple-element.14, s32[192]{0:T(256)S(1)} %get-tuple-element.17, s32[]{:T(128)S(6)} %mul.58, s32[192]{0:T(256)S(1)} %get-tuple-element.13, s32[192]{0:T(256)S(1)} %get-tuple-element.18, ...), kind=kOutput, calls=%fused_computation.3 | convolution fusion | flops 681025536 | bytes 5902852 | tf_op jit(solution)/shard_map/ij,jbr->bir/dot_general | solution.py:57
  116.1 4.7 %all-to-all-start.2 = ((bf16[24,288,128]{2,1,0:T(8,128)(2,1)}), bf16[24,288,128]{2,1,0:T(8,128)(2,1)}, u32[]{:S(2)}, u32[]{:S(2)}) async-start(bf16[24,288,128]{2,1,0:T(8,128)(2,1)} %convert_bitcast_fusion), calls=%async_computation.2 | async-start | bytes 3538944 | tf_op jit(solution)/shard_map/all_to_all | solution.py:63
  120.9 59.3 %all-to-all-done.2 = bf16[24,288,128]{2,1,0:T(8,128)(2,1)} async-done(((bf16[24,288,128]{2,1,0:T(8,128)(2,1)}), bf16[24,288,128]{2,1,0:T(8,128)(2,1)}, u32[]{:S(2)}, u32[]{:S(2)}) %all-to-all-start.2) | async-done | bytes 1769504 | tf_op jit(solution)/shard_map/all_to_all | solution.py:63
  180.2 1.7 convert_reduce_fusion
  181.9 4.4 %collective-permute-start.2 = (f32[144,128]{1,0:T(8,128)S(1)}, f32[144,128]{1,0:T(8,128)S(1)}, u32[]{:S(2)}, u32[]{:S(2)}) collective-permute-start(f32[144,128]{1,0:T(8,128)S(1)} %slice_select_fusion), channel_id=1, source_target_pairs={{0,1},{1,0},{2,3},{3,2},{4,5},{5,4},{6,7},{7,6},{8,9},{9,8},{10,11... | collective-permute-start | bytes 221192 | tf_op jit(solution)/shard_map/ppermute | solution.py:68
  186.3 0.9 collective-permute-done.2
  187.2 0.8 pad_maximum_fusion.1
  (16 shorter events, 0.2 us)
Async XLA Ops:
  6.5 1.6 copy-start
  6.5 101.4 %all-gather.3.cloned.1.call-start = ((), (), s32[]{:S(2)}) async-start(), calls=%async_computation.3 | async-start | bytes 1916928 | tf_op jit(solution)/shard_map/all_gather | solution.py:44
  40.9 5.4 %collective-permute-start.1 = (bf16[12,3072]{1,0:T(8,128)(2,1)S(1)}, bf16[12,3072]{1,0:T(8,128)(2,1)S(1)}, u32[]{:S(2)}, u32[]{:S(2)}) collective-permute-start(bf16[12,3072]{1,0:T(8,128)(2,1)S(1)} %bitcast.26), channel_id=1, source_target_pairs={{0,24},{24,0},{1,25},{25,1},{2,26},{26,2},{3,27},{27,3},{4,28},{28... | collective-permute-start | bytes 221192 | tf_op jit(solution)/shard_map/ppermute | solution.py:41
  47.2 7.2 %collective-permute-start = (bf16[12,3072]{1,0:T(8,128)(2,1)S(1)}, bf16[12,3072]{1,0:T(8,128)(2,1)S(1)}, u32[]{:S(2)}, u32[]{:S(2)}) collective-permute-start(bf16[12,3072]{1,0:T(8,128)(2,1)S(1)} %bitcast.28), channel_id=1, source_target_pairs={{0,1},{1,0},{2,3},{3,2},{4,5},{5,4},{6,7},{7,6},{8,9},{9,8},{10,11... | collective-permute-start | bytes 221192 | tf_op jit(solution)/shard_map/ppermute | solution.py:40
  55.7 47.3 %all-to-all-start.1 = ((bf16[16,12,3072]{2,1,0:T(8,128)(2,1)}), bf16[16,12,3072]{2,1,0:T(8,128)(2,1)}, u32[]{:S(2)}, u32[]{:S(2)}) async-start(bf16[16,12,3072]{2,1,0:T(8,128)(2,1)} %broadcast_in_dim.2), calls=%async_computation.1 | async-start | bytes 3145728 | tf_op jit(solution)/shard_map/all_to_all | solution.py:16
  116.1 64.0 %all-to-all-start.2 = ((bf16[24,288,128]{2,1,0:T(8,128)(2,1)}), bf16[24,288,128]{2,1,0:T(8,128)(2,1)}, u32[]{:S(2)}, u32[]{:S(2)}) async-start(bf16[24,288,128]{2,1,0:T(8,128)(2,1)} %convert_bitcast_fusion), calls=%async_computation.2 | async-start | bytes 3538944 | tf_op jit(solution)/shard_map/all_to_all | solution.py:63
  181.9 5.3 %collective-permute-start.2 = (f32[144,128]{1,0:T(8,128)S(1)}, f32[144,128]{1,0:T(8,128)S(1)}, u32[]{:S(2)}, u32[]{:S(2)}) collective-permute-start(f32[144,128]{1,0:T(8,128)S(1)} %slice_select_fusion), channel_id=1, source_target_pairs={{0,1},{1,0},{2,3},{3,2},{4,5},{5,4},{6,7},{7,6},{8,9},{9,8},{10,11... | collective-permute-start | bytes 221192 | tf_op jit(solution)/shard_map/ppermute | solution.py:68
Sparse Core Ops, SparseCore 0:
  47.3 54.0 all-gather.2

commit v2 on v1

v2 whole, which is shorter than its diff:
```python
import jax
import jax.numpy as jnp
from jax import lax
from jax.experimental import pallas as pl
from jax.experimental.pallas import tpu as pltpu
from jax.sharding import Mesh
from jax.sharding import PartitionSpec as P

epsilon = 1e-05
off_weight = 0.0051
batch_axes = ("x_lo", "z")
feat_axes = ("x_hi", "y")
bf16, f32 = jnp.bfloat16, jnp.float32
swap = [(0, 1), (1, 0)]


def spread(part, axes):
    copies = jnp.broadcast_to(part[None], (lax.axis_size(axes),) + part.shape)
    return lax.all_to_all(copies, axes, 0, 0, tiled=True)


def product_kernel(grad_ref, other_ref, out_ref):
    rows_here = out_ref.shape[2]
    for block in range(out_ref.shape[0]):
        out_ref[block] = jnp.dot(
            grad_ref[...],
            other_ref[:, block * rows_here : (block + 1) * rows_here],
            preferred_element_type=f32,
        ).astype(bf16)


def products(grad, other, rows_here):
    blocks = other.shape[1] // rows_here
    return pl.pallas_call(
        product_kernel,
        out_shape=jax.ShapeDtypeStruct((blocks, grad.shape[0], rows_here), bf16),
        in_specs=[pl.BlockSpec(memory_space=pltpu.VMEM)] * 2,
        out_specs=pl.BlockSpec(memory_space=pltpu.VMEM),
        compiler_params=pltpu.CompilerParams(vmem_limit_bytes=24 * 2**20),
    )(grad, other)


def shards(hidden_act, proj_weight):
    depth = lax.axis_size("z")
    view_rows = hidden_act[0]
    rows_here = view_rows.shape[0]
    half_rows = rows_here * depth
    row_total = half_rows * lax.axis_size("x_lo")
    feat_here = proj_weight.shape[1]
    own = feat_here // depth
    twin = lax.axis_index("twin")
    projected = lax.dot_general(
        proj_weight, view_rows, (((0,), (1,)), ((), ())), preferred_element_type=f32
    )
    projected = lax.optimization_barrier(projected)
    by_rows = lax.all_to_all(
        projected.reshape(depth, own, rows_here), "z", 0, 0, tiled=True
    )
    sums = jnp.stack(
        [jnp.sum(by_rows, axis=(0, 2)), jnp.sum(by_rows * by_rows, axis=(0, 2))]
    )
    sums = sums + lax.ppermute(sums, "x_lo", swap)
    feat_mean = (sums[0] / row_total)[None, :, None]
    feat_var = (sums[1] / row_total)[None, :, None] - feat_mean * feat_mean
    normed = ((by_rows - feat_mean) * lax.rsqrt(feat_var + epsilon)).astype(bf16)
    normed = normed.transpose(1, 0, 2).reshape(own, half_rows)
    far = lax.ppermute(normed, "x_hi", swap)
    other = lax.ppermute(normed, "twin", swap)
    low = lax.axis_index("x_hi") == 0
    pair = jnp.concatenate([jnp.where(low, normed, far), jnp.where(low, far, normed)])
    there = lax.all_gather(pair, "y", axis=0, tiled=True)
    here = spread(other, "z").reshape(feat_here, half_rows)
    corr = lax.dot_general(
        here, there, (((1,), (1,)), ((), ())), preferred_element_type=f32
    )
    corr = (corr + lax.ppermute(corr, "x_lo", swap)) / row_total
    row_ids = lax.broadcasted_iota(jnp.int32, corr.shape, 0)
    row_ids = row_ids + lax.axis_index(feat_axes) * feat_here
    cols = lax.broadcasted_iota(jnp.int32, corr.shape, 1)
    chunks = cols // own
    col_feats = (chunks % 2) * lax.axis_size("y") + chunks // 2
    col_ids = col_feats * feat_here + lax.axis_index("z") * own + cols % own
    grad = jnp.where(
        row_ids == col_ids, -2.0 * (1.0 - corr), 2.0 * off_weight * corr
    ).astype(bf16)
    terms = lax.all_to_all(products(grad, there, rows_here), "z", 0, 0, tiled=True)
    total = jnp.sum(terms.astype(f32), axis=0)
    first, second = jnp.split(total, 2, axis=0)
    keep = jnp.where(twin == 0, first, second)
    give = jnp.where(twin == 0, second, first)
    take = lax.ppermute(give, "twin", swap)
    return jnp.stack(
        [jnp.where(twin == 0, take, keep), jnp.where(twin == 0, keep, take)], axis=1
    )


def solution(mesh):
    parts = 2
    shape = mesh.devices.shape
    fine = Mesh(
        mesh.devices.reshape(
            parts, shape[0] // parts, parts, shape[1] // parts, shape[2]
        ),
        ("x_hi", "y", "x_lo", "z", "twin"),
    )
    return jax.shard_map(
        shards,
        mesh=fine,
        in_specs=(P("twin", batch_axes, None), P(None, feat_axes)),
        out_specs=P(feat_axes + ("twin",), None, batch_axes),
        check_vma=False,
    )
```

time: 195 us -> 171 us (0.88)
  waiting for transfers between devices: 102 us -> 78.5 us
  starting transfers between devices: 26.7 us -> 38.9 us
  local copies, waits for them, and re-layouts: 11.8 us -> 3.5 us
  matrix products: 8.79 us -> 5.97 us
    all_gather x1, waiting for transfers between devices: 0.01 us -> 41.1 us  [shards(): there = lax.all_gather(pair, 'y', axis=0, tiled=True)]
    all_to_all x1, waiting for transfers between devices: 38.1 us -> 0.01 us  [spread(): return lax.all_to_all(copies, axes, 0, 0, tiled=True)]
    all_to_all x1, waiting for transfers between devices: 59.3 us -> 29.6 us  [shards(): lax.all_to_all(products(grad, there, rows_here), 'z', 0, 0, tiled=True)]
    ppermute x3 -> x5, starting transfers between devices: 12.8 us -> 24 us  [the longest x1 7.17 us: shards(): take = lax.ppermute(give, 'twin', swap)]
    all_to_all x1, starting transfers between devices: 4.74 us -> 10.5 us  [shards(): lax.all_to_all(products(grad, there, rows_here), 'z', 0, 0, tiled=True)]
    all_to_all x1, starting transfers between devices: 9.14 us -> 4.37 us  [spread(): return lax.all_to_all(copies, axes, 0, 0, tiled=True)]
    another operation x2 -> x0, local copies, waits for them, and re-layouts: 4.22 us -> none  [the longest x1 3.4 us: shards(): there.reshape(feats * own, batches, rows_here)]
    all_gather x1 -> x0, local copies, waits for them, and re-layouts: 3.07 us -> none  [shards(): here = lax.all_gather(pair, 'z', axis=1)]
  transfers between devices with their start and end apart: 6 -> 8, of which waited for: 5 -> 5; matrix products, arithmetic and copies ran while one was open for 3% -> 1% of each run, Pallas kernels for 0% -> 0%
where the time goes in v2:
time: 171 us; the launch traced here: 170 us
  waiting for transfers between devices  78.5 us (46%)
  starting transfers between devices  38.9 us (23%)
  blocking collectives  26.9 us (16%)
  between operations  13.6 us (8%)
  matrix products  5.97 us (3%)
  local copies, waits for them, and re-layouts  3.5 us (2%)
  other arithmetic  2.15 us (1%)
    all_gather x1, waiting for transfers between devices, shards(): there = lax.all_gather(pair, 'y', axis=0, tiled=True)  41.1 us
    all_to_all x1, waiting for transfers between devices, shards(): lax.all_to_all(products(grad, there, rows_here), 'z', 0, 0, tiled=True)  29.6 us
    all_to_all x1, blocking collectives, shards(): lax.all_to_all(projected.reshape(depth, own, rows_here), 'z', 0, 0, tiled...  26.9 us
    all_to_all x1, starting transfers between devices, shards(): lax.all_to_all(products(grad, there, rows_here), 'z', 0, 0, tiled=True)  10.5 us
    ppermute x1, starting transfers between devices, shards(): take = lax.ppermute(give, 'twin', swap)  7.17 us
    ppermute x1, waiting for transfers between devices, shards(): corr = (corr + lax.ppermute(corr, 'x_lo', swap)) / row_total  5.62 us
    ppermute x1, starting transfers between devices, shards(): other = lax.ppermute(normed, 'twin', swap)  5.51 us
    ppermute x1, starting transfers between devices, shards(): far = lax.ppermute(normed, 'x_hi', swap)  4.66 us
  transfers between devices with their start and end apart: 8, of which 5 were waited for; matrix products, arithmetic and copies ran while one was open for 1% of the time, Pallas kernels for 0%

profile of v2, /device:TPU:1, one launch (start us, length us, event | category | flops | bytes accessed | tf_op | source)
XLA Modules:
  0.0 170.3 jit_solution(1198364851032076087)
XLA Ops:
  6.5 1.6 copy-done
  8.1 3.7 %fusion = f32[288,128]{1,0:T(8,128)S(1)} fusion(bf16[8192,288]{0,1:T(8,128)(2,1)} %param.3, bf16[1,128,8192]{2,1,0:T(8,128)(2,1)S(1)} %copy-done), kind=kOutput, calls=%fused_computation | convolution fusion | flops 603979776 | bytes 6963200 | tf_op jit(solution)/shard_map/dot_general | solution.py:52
  11.8 26.9 %all_to_all.15 = f32[12,24,128]{2,1,0:T(8,128)S(1)} all-to-all(f32[12,24,128]{2,1,0:T(8,128)S(1)} %bitcast.35), channel_id=1, replica_groups=mesh['x_hi'=2,'y'=8,'x_lo'=2,'z'=12,'twin'=2] {'z'}, dimensions={0} | all-to-all | bytes 294912 | tf_op jit(solution)/shard_map/all_to_all | solution.py:56
  38.7 0.1 fusion.22
  38.8 3.1 %collective-permute-start = (f32[2,24]{1,0:T(2,128)S(1)}, f32[2,24]{1,0:T(2,128)S(1)}, u32[]{:S(2)}, u32[]{:S(2)}) collective-permute-start(f32[2,24]{1,0:T(2,128)S(1)} %pad_maximum_fusion.2), channel_id=1, source_target_pairs={{0,24},{24,0},{1,25},{25,1},{2,26},{26,2},{3,27},{27,3},{4,28},{28... | collective-permute-start | bytes 584 | tf_op jit(solution)/shard_map/ppermute | solution.py:62
  42.0 1.2 collective-permute-done
  43.3 5.5 %collective-permute-start.1 = (bf16[24,1536]{1,0:T(8,128)(2,1)S(1)}, bf16[24,1536]{1,0:T(8,128)(2,1)S(1)}, u32[]{:S(2)}, u32[]{:S(2)}) collective-permute-start(bf16[24,1536]{1,0:T(8,128)(2,1)S(1)} %copy_bitcast_fusion), channel_id=1, source_target_pairs={{0,1},{1,0},{2,3},{3,2},{4,5},{5,4},{6,7},{7,6},{8,9},{9,8},{10,11... | collective-permute-start | bytes 221192 | tf_op jit(solution)/shard_map/ppermute | solution.py:68
  48.8 4.7 %collective-permute-start.2 = (bf16[24,1536]{1,0:T(8,128)(2,1)S(1)}, bf16[24,1536]{1,0:T(8,128)(2,1)S(1)}, u32[]{:S(2)}, u32[]{:S(2)}) collective-permute-start(bf16[24,1536]{1,0:T(8,128)(2,1)S(1)} %copy_bitcast_fusion), channel_id=1, source_target_pairs={{0,384},{384,0},{1,385},{385,1},{2,386},{386,2},{3,387},{387,3},{4... | collective-permute-start | bytes 221192 | tf_op jit(solution)/shard_map/ppermute | solution.py:67
  53.5 1.0 broadcast_in_dim.2
  54.5 4.4 %all-to-all-start.1 = ((bf16[12,24,1536]{2,1,0:T(8,128)(2,1)}), bf16[12,24,1536]{2,1,0:T(8,128)(2,1)}, u32[]{:S(2)}, u32[]{:S(2)}) async-start(bf16[12,24,1536]{2,1,0:T(8,128)(2,1)} %broadcast_in_dim.2), calls=%async_computation.1 | async-start | bytes 1769472 | tf_op jit(solution)/shard_map/all_to_all | solution.py:19
  59.0 0.7 pad_maximum_fusion
  59.7 41.1 %all-gather.2.cloned.1.call-done.other_ref = bf16[384,1536]{1,0:T(8,128)(2,1)} async-done(((bf16[48,1536]{1,0:T(8,128)(2,1)}), bf16[384,1536]{1,0:T(8,128)(2,1)}) %all-gather.2.cloned.1.call-update) | async-done | bytes 1179664 | tf_op jit(solution)/shard_map/all_gather | solution.py:71
  100.8 2.3 %fusion.23 = f32[288,384]{1,0:T(8,128)S(1)} fusion(bf16[288,1536]{1,0:T(8,128)(2,1)} %bitcast.7, bf16[384,1536]{1,0:T(8,128)(2,1)} %all-gather.2.cloned.1.call-done.other_ref), kind=kOutput, calls=%fused_computation.52 | convolution fusion | flops 339738624 | bytes 2506752 | tf_op jit(solution)/shard_map/dot_general | solution.py:73
  103.1 3.5 %collective-permute-start.3 = (f32[288,384]{1,0:T(8,128)S(1)}, f32[288,384]{1,0:T(8,128)S(1)}, u32[]{:S(2)}, u32[]{:S(2)}) collective-permute-start(f32[288,384]{1,0:T(8,128)S(1)} %fusion.23), channel_id=1, source_target_pairs={{0,24},{24,0},{1,25},{25,1},{2,26},{26,2},{3,27},{27,3},{4,28},{28... | collective-permute-start | bytes 1327112 | tf_op jit(solution)/shard_map/ppermute | solution.py:76
  106.7 5.6 %collective-permute-done.3 = f32[288,384]{1,0:T(8,128)S(1)} collective-permute-done((f32[288,384]{1,0:T(8,128)S(1)}, f32[288,384]{1,0:T(8,128)S(1)}, u32[]{:S(2)}, u32[]{:S(2)}) %collective-permute-start.3) | collective-permute-done | bytes 442400 | tf_op jit(solution)/shard_map/ppermute | solution.py:76
  112.3 0.2 select_convert_fusion.grad_ref
  112.5 0.9 shard_map.28
  113.4 0.9 copy-done.2
  114.3 10.5 %all-to-all-start.2 = ((bf16[12,288,128]{2,1,0:T(8,128)(2,1)}), bf16[12,288,128]{2,1,0:T(8,128)(2,1)S(1)}, u32[]{:S(2)}, u32[]{:S(2)}) async-start(bf16[12,288,128]{2,1,0:T(8,128)(2,1)} %copy-done.2), calls=%async_computation.2 | async-start | bytes 1769472 | tf_op jit(solution)/shard_map/all_to_all | solution.py:86
  124.8 29.6 %all-to-all-done.2 = bf16[12,288,128]{2,1,0:T(8,128)(2,1)S(1)} async-done(((bf16[12,288,128]{2,1,0:T(8,128)(2,1)}), bf16[12,288,128]{2,1,0:T(8,128)(2,1)S(1)}, u32[]{:S(2)}, u32[]{:S(2)}) %all-to-all-start.2) | async-done | bytes 884768 | tf_op jit(solution)/shard_map/all_to_all | solution.py:86
  154.5 0.1 convert_reduce_fusion
  154.6 7.2 %collective-permute-start.4 = (f32[144,128]{1,0:T(8,128)S(1)}, f32[144,128]{1,0:T(8,128)S(1)}, u32[]{:S(2)}, u32[]{:S(2)}) collective-permute-start(f32[144,128]{1,0:T(8,128)S(1)} %slice_select_fusion.1), channel_id=1, source_target_pairs={{0,1},{1,0},{2,3},{3,2},{4,5},{5,4},{6,7},{7,6},{8,9},{9,8},{10,11... | collective-permute-start | bytes 221192 | tf_op jit(solution)/shard_map/ppermute | solution.py:91
  161.8 0.9 collective-permute-done.4
  162.7 0.8 pad_maximum_fusion.1
  (21 shorter events, 0.4 us)
Async XLA Ops:
  6.5 1.6 copy-start
  38.8 4.3 %collective-permute-start = (f32[2,24]{1,0:T(2,128)S(1)}, f32[2,24]{1,0:T(2,128)S(1)}, u32[]{:S(2)}, u32[]{:S(2)}) collective-permute-start(f32[2,24]{1,0:T(2,128)S(1)} %pad_maximum_fusion.2), channel_id=1, source_target_pairs={{0,24},{24,0},{1,25},{25,1},{2,26},{26,2},{3,27},{27,3},{4,28},{28... | collective-permute-start | bytes 584 | tf_op jit(solution)/shard_map/ppermute | solution.py:62
  43.3 10.2 %collective-permute-start.1 = (bf16[24,1536]{1,0:T(8,128)(2,1)S(1)}, bf16[24,1536]{1,0:T(8,128)(2,1)S(1)}, u32[]{:S(2)}, u32[]{:S(2)}) collective-permute-start(bf16[24,1536]{1,0:T(8,128)(2,1)S(1)} %copy_bitcast_fusion), channel_id=1, source_target_pairs={{0,1},{1,0},{2,3},{3,2},{4,5},{5,4},{6,7},{7,6},{8,9},{9,8},{10,11... | collective-permute-start | bytes 221192 | tf_op jit(solution)/shard_map/ppermute | solution.py:68
  48.8 10.1 %collective-permute-start.2 = (bf16[24,1536]{1,0:T(8,128)(2,1)S(1)}, bf16[24,1536]{1,0:T(8,128)(2,1)S(1)}, u32[]{:S(2)}, u32[]{:S(2)}) collective-permute-start(bf16[24,1536]{1,0:T(8,128)(2,1)S(1)} %copy_bitcast_fusion), channel_id=1, source_target_pairs={{0,384},{384,0},{1,385},{385,1},{2,386},{386,2},{3,387},{387,3},{4... | collective-permute-start | bytes 221192 | tf_op jit(solution)/shard_map/ppermute | solution.py:67
  54.5 46.4 %all-to-all-start.1 = ((bf16[12,24,1536]{2,1,0:T(8,128)(2,1)}), bf16[12,24,1536]{2,1,0:T(8,128)(2,1)}, u32[]{:S(2)}, u32[]{:S(2)}) async-start(bf16[12,24,1536]{2,1,0:T(8,128)(2,1)} %broadcast_in_dim.2), calls=%async_computation.1 | async-start | bytes 1769472 | tf_op jit(solution)/shard_map/all_to_all | solution.py:19
  58.9 42.0 %all-gather.2.cloned.1.call-start = ((), (), s32[]{:S(2)}) async-start(), calls=%async_computation.3 | async-start | bytes 1327104 | tf_op jit(solution)/shard_map/all_gather | solution.py:71
  100.8 11.7 %copy-start.1 = (bf16[384,1536]{1,0:T(8,128)(2,1)S(1)}, bf16[384,1536]{1,0:T(8,128)(2,1)}, u32[]{:S(2)}) copy-start(bf16[384,1536]{1,0:T(8,128)(2,1)} %all-gather.2.cloned.1.call-done.other_ref) | copy-start | bytes 3538948
  103.1 9.2 %collective-permute-start.3 = (f32[288,384]{1,0:T(8,128)S(1)}, f32[288,384]{1,0:T(8,128)S(1)}, u32[]{:S(2)}, u32[]{:S(2)}) collective-permute-start(f32[288,384]{1,0:T(8,128)S(1)} %fusion.23), channel_id=1, source_target_pairs={{0,24},{24,0},{1,25},{25,1},{2,26},{26,2},{3,27},{27,3},{4,28},{28... | collective-permute-start | bytes 1327112 | tf_op jit(solution)/shard_map/ppermute | solution.py:76
  113.3 0.9 copy-start.2
  114.3 40.2 %all-to-all-start.2 = ((bf16[12,288,128]{2,1,0:T(8,128)(2,1)}), bf16[12,288,128]{2,1,0:T(8,128)(2,1)S(1)}, u32[]{:S(2)}, u32[]{:S(2)}) async-start(bf16[12,288,128]{2,1,0:T(8,128)(2,1)} %copy-done.2), calls=%async_computation.2 | async-start | bytes 1769472 | tf_op jit(solution)/shard_map/all_to_all | solution.py:86
  154.6 8.1 %collective-permute-start.4 = (f32[144,128]{1,0:T(8,128)S(1)}, f32[144,128]{1,0:T(8,128)S(1)}, u32[]{:S(2)}, u32[]{:S(2)}) collective-permute-start(f32[144,128]{1,0:T(8,128)S(1)} %slice_select_fusion.1), channel_id=1, source_target_pairs={{0,1},{1,0},{2,3},{3,2},{4,5},{5,4},{6,7},{7,6},{8,9},{9,8},{10,11... | collective-permute-start | bytes 221192 | tf_op jit(solution)/shard_map/ppermute | solution.py:91
Sparse Core Ops, SparseCore 0:
  62.1 38.7 all-gather.1

commit v3 on v2

--- a/solution.py
+++ b/solution.py
@@ -41,7 +41,7 @@
 
 
 def shards(hidden_act, proj_weight):
-    depth = lax.axis_size("z")
+    depth, feats = lax.axis_size("z"), lax.axis_size(feat_axes)
     view_rows = hidden_act[0]
     rows_here = view_rows.shape[0]
     half_rows = rows_here * depth
@@ -59,17 +59,14 @@
     sums = jnp.stack(
         [jnp.sum(by_rows, axis=(0, 2)), jnp.sum(by_rows * by_rows, axis=(0, 2))]
     )
-    sums = sums + lax.ppermute(sums, "x_lo", swap)
+    sums = lax.psum(sums, "x_lo")
     feat_mean = (sums[0] / row_total)[None, :, None]
     feat_var = (sums[1] / row_total)[None, :, None] - feat_mean * feat_mean
     normed = ((by_rows - feat_mean) * lax.rsqrt(feat_var + epsilon)).astype(bf16)
     normed = normed.transpose(1, 0, 2).reshape(own, half_rows)
-    far = lax.ppermute(normed, "x_hi", swap)
     other = lax.ppermute(normed, "twin", swap)
-    low = lax.axis_index("x_hi") == 0
-    pair = jnp.concatenate([jnp.where(low, normed, far), jnp.where(low, far, normed)])
-    there = lax.all_gather(pair, "y", axis=0, tiled=True)
-    here = spread(other, "z").reshape(feat_here, half_rows)
+    there = spread(normed, feat_axes).reshape(feats * own, half_rows)
+    here = lax.all_gather(other, "z", axis=0, tiled=True)
     corr = lax.dot_general(
         here, there, (((1,), (1,)), ((), ())), preferred_element_type=f32
     )
@@ -77,9 +74,7 @@
     row_ids = lax.broadcasted_iota(jnp.int32, corr.shape, 0)
     row_ids = row_ids + lax.axis_index(feat_axes) * feat_here
     cols = lax.broadcasted_iota(jnp.int32, corr.shape, 1)
-    chunks = cols // own
-    col_feats = (chunks % 2) * lax.axis_size("y") + chunks // 2
-    col_ids = col_feats * feat_here + lax.axis_index("z") * own + cols % own
+    col_ids = (cols // own) * feat_here + lax.axis_index("z") * own + cols % own
     grad = jnp.where(
         row_ids == col_ids, -2.0 * (1.0 - corr), 2.0 * off_weight * corr
     ).astype(bf16)

time: 171 us -> 135 us (0.79)
  waiting for transfers between devices: 78.5 us -> 39 us
  blocking collectives: 26.9 us -> 54.4 us
  between operations: 13.6 us -> 0.15 us
  starting transfers between devices: 38.9 us -> 28 us
    all_gather x1 -> x0, waiting for transfers between devices: 41.1 us -> none  [shards(): there = lax.all_gather(pair, 'y', axis=0, tiled=True)]
    all_gather x0 -> x1, blocking collectives: none -> 23.8 us  [shards(): here = lax.all_gather(other, 'z', axis=0, tiled=True)]
    ppermute x2 -> x0, starting transfers between devices: 7.78 us -> none  [the longest x1 4.66 us: shards(): far = lax.ppermute(normed, 'x_hi', swap)]
    all_to_all x1, starting transfers between devices: 10.5 us -> 3.69 us  [shards(): lax.all_to_all(products(grad, there, rows_here), 'z', 0, 0, tiled=True)]
    all_to_all x1, starting transfers between devices: 4.37 us -> 9.39 us  [spread(): return lax.all_to_all(copies, axes, 0, 0, tiled=True)]
    psum x0 -> x1, blocking collectives: none -> 3.8 us  [shards(): sums = lax.psum(sums, 'x_lo')]
    ppermute x1, waiting for transfers between devices: 5.62 us -> 7.61 us  [shards(): corr = (corr + lax.ppermute(corr, 'x_lo', swap)) / row_total]
  transfers between devices with their start and end apart: 8 -> 5, of which waited for: 5 -> 4; matrix products, arithmetic and copies ran while one was open for 1% -> 0% of each run, Pallas kernels for 0% -> 0%
where the time goes in v3:
time: 135 us; the launch traced here: 133 us
  blocking collectives  54.4 us (40%)
  waiting for transfers between devices  39 us (29%)
  starting transfers between devices  28 us (21%)
  matrix products  5.51 us (4%)
  local copies, waits for them, and re-layouts  3.6 us (3%)
  other arithmetic  1.36 us (1%)
    all_to_all x1, waiting for transfers between devices, shards(): lax.all_to_all(products(grad, there, rows_here), 'z', 0, 0, tiled=True)  29.6 us
    all_to_all x1, blocking collectives, shards(): lax.all_to_all(projected.reshape(depth, own, rows_here), 'z', 0, 0, tiled...  26.9 us
    all_gather x1, blocking collectives, shards(): here = lax.all_gather(other, 'z', axis=0, tiled=True)  23.8 us
    all_to_all x1, starting transfers between devices, spread(): return lax.all_to_all(copies, axes, 0, 0, tiled=True)  9.39 us
    ppermute x1, waiting for transfers between devices, shards(): corr = (corr + lax.ppermute(corr, 'x_lo', swap)) / row_total  7.61 us
    ppermute x1, starting transfers between devices, shards(): take = lax.ppermute(give, 'twin', swap)  6.89 us
    ppermute x1, starting transfers between devices, shards(): other = lax.ppermute(normed, 'twin', swap)  5.79 us
    psum x1, blocking collectives, shards(): sums = lax.psum(sums, 'x_lo')  3.8 us
  transfers between devices with their start and end apart: 5, of which 4 were waited for; matrix products, arithmetic and copies ran while one was open for 0% of the time, Pallas kernels for 0%

profile of v3, /device:TPU:1, one launch (start us, length us, event | category | flops | bytes accessed | tf_op | source)
XLA Modules:
  0.0 132.9 jit_solution(10629030232681758815)
XLA Ops:
  0.0 1.6 %copy-done = bf16[1,128,8192]{2,1,0:T(8,128)(2,1)S(1)} copy-done((bf16[1,128,8192]{2,1,0:T(8,128)(2,1)S(1)}, bf16[1,128,8192]{2,1,0:T(8,128)(2,1)}, u32[]{:S(2)}) %copy-start) | copy-done | bytes 2097176
  1.6 3.7 %fusion = f32[288,128]{1,0:T(8,128)S(1)} fusion(bf16[8192,288]{0,1:T(8,128)(2,1)} %param.3, bf16[1,128,8192]{2,1,0:T(8,128)(2,1)S(1)} %copy-done), kind=kOutput, calls=%fused_computation | convolution fusion | flops 603979776 | bytes 6963200 | tf_op jit(solution)/shard_map/dot_general | solution.py:52
  5.3 26.9 %all_to_all.15 = f32[12,24,128]{2,1,0:T(8,128)S(1)} all-to-all(f32[12,24,128]{2,1,0:T(8,128)S(1)} %bitcast.32), channel_id=1, replica_groups=mesh['x_hi'=2,'y'=8,'x_lo'=2,'z'=12,'twin'=2] {'z'}, dimensions={0} | all-to-all | bytes 294912 | tf_op jit(solution)/shard_map/all_to_all | solution.py:56
  32.2 0.1 fusion.11
  32.3 3.8 %psum.7 = f32[2,24]{1,0:T(2,128)S(1)} all-reduce(f32[2,24]{1,0:T(2,128)S(1)} %pad_maximum_fusion.1), channel_id=1, replica_groups=mesh['x_hi'=2,'y'=8,'x_lo'=2,'z'=12,'twin'=2] {'x_lo'}, use_global_device_ids=true, to_apply=%region_2.0 | all-reduce | flops 48 | bytes 384 | tf_op jit(solution)/shard_map/psum | solution.py:62
  36.1 0.1 copy_bitcast_fusion
  36.2 1.1 broadcast_in_dim.2
  37.3 9.4 %all-to-all-start.1 = ((bf16[16,24,1536]{2,1,0:T(8,128)(2,1)}), bf16[16,24,1536]{2,1,0:T(8,128)(2,1)S(1)}, u32[]{:S(2)}, u32[]{:S(2)}) async-start(bf16[16,24,1536]{2,1,0:T(8,128)(2,1)} %broadcast_in_dim.2), calls=%async_computation.1 | async-start | bytes 2359296 | tf_op jit(solution)/shard_map/all_to_all | solution.py:19
  46.7 5.8 %collective-permute-start = (bf16[24,1536]{1,0:T(8,128)(2,1)S(1)}, bf16[24,1536]{1,0:T(8,128)(2,1)S(1)}, u32[]{:S(2)}, u32[]{:S(2)}) collective-permute-start(bf16[24,1536]{1,0:T(8,128)(2,1)S(1)} %copy_bitcast_fusion), channel_id=1, source_target_pairs={{0,1},{1,0},{2,3},{3,2},{4,5},{5,4},{6,7},{7,6},{8,9},{9,8},{10,11... | collective-permute-start | bytes 221192 | tf_op jit(solution)/shard_map/ppermute | solution.py:67
  52.5 0.9 collective-permute-done
  53.4 23.8 %all_gather.3 = bf16[288,1536]{1,0:T(8,128)(2,1)} all-gather(bf16[24,1536]{1,0:T(8,128)(2,1)S(1)} %collective-permute-done), channel_id=1, replica_groups=mesh['x_hi'=2,'y'=8,'x_lo'=2,'z'=12,'twin'=2] {'z'}, dimensions={0}, use_global_device_ids=true | all-gather | bytes 958464 | tf_op jit(solution)/shard_map/all_gather | solution.py:69
  77.2 0.0 all-to-all-done.1
  77.2 1.8 %fusion.12 = f32[288,384]{1,0:T(8,128)S(1)} fusion(bf16[288,1536]{1,0:T(8,128)(2,1)} %all_gather.3, bf16[384,1536]{1,0:T(8,128)(2,1)S(1)} %bitcast.30), kind=kOutput, calls=%fused_computation.31 | convolution fusion | flops 339738624 | bytes 2506752 | tf_op jit(solution)/shard_map/dot_general | solution.py:70
  79.0 2.2 %collective-permute-start.1 = (f32[288,384]{1,0:T(8,128)S(1)}, f32[288,384]{1,0:T(8,128)S(1)}, u32[]{:S(2)}, u32[]{:S(2)}) collective-permute-start(f32[288,384]{1,0:T(8,128)S(1)} %fusion.12), channel_id=1, source_target_pairs={{0,24},{24,0},{1,25},{25,1},{2,26},{26,2},{3,27},{27,3},{4,28},{28... | collective-permute-start | bytes 1327112 | tf_op jit(solution)/shard_map/ppermute | solution.py:73
  81.3 7.6 %collective-permute-done.1 = f32[288,384]{1,0:T(8,128)S(1)} collective-permute-done((f32[288,384]{1,0:T(8,128)S(1)}, f32[288,384]{1,0:T(8,128)S(1)}, u32[]{:S(2)}, u32[]{:S(2)}) %collective-permute-start.1) | collective-permute-done | bytes 442400 | tf_op jit(solution)/shard_map/ppermute | solution.py:73
  88.9 0.1 select_convert_fusion.grad_ref
  89.1 0.9 shard_map.28
  89.9 0.9 copy-done.1
  90.8 3.7 %all-to-all-start.2 = ((bf16[12,288,128]{2,1,0:T(8,128)(2,1)}), bf16[12,288,128]{2,1,0:T(8,128)(2,1)S(1)}, u32[]{:S(2)}, u32[]{:S(2)}) async-start(bf16[12,288,128]{2,1,0:T(8,128)(2,1)} %copy-done.1), calls=%async_computation.2 | async-start | bytes 1769472 | tf_op jit(solution)/shard_map/all_to_all | solution.py:81
  94.5 29.6 %all-to-all-done.2 = bf16[12,288,128]{2,1,0:T(8,128)(2,1)S(1)} async-done(((bf16[12,288,128]{2,1,0:T(8,128)(2,1)}), bf16[12,288,128]{2,1,0:T(8,128)(2,1)S(1)}, u32[]{:S(2)}, u32[]{:S(2)}) %all-to-all-start.2) | async-done | bytes 884768 | tf_op jit(solution)/shard_map/all_to_all | solution.py:81
  124.1 0.1 convert_reduce_fusion
  124.3 6.9 %collective-permute-start.2 = (f32[144,128]{1,0:T(8,128)S(1)}, f32[144,128]{1,0:T(8,128)S(1)}, u32[]{:S(2)}, u32[]{:S(2)}) collective-permute-start(f32[144,128]{1,0:T(8,128)S(1)} %slice_select_fusion.1), channel_id=1, source_target_pairs={{0,1},{1,0},{2,3},{3,2},{4,5},{5,4},{6,7},{7,6},{8,9},{9,8},{10,11... | collective-permute-start | bytes 221192 | tf_op jit(solution)/shard_map/ppermute | solution.py:86
  131.2 0.9 collective-permute-done.2
  132.1 0.8 pad_maximum_fusion
  (11 shorter events, 0.1 us)
Async XLA Ops:
  0.0 1.6 %copy-start = (bf16[1,128,8192]{2,1,0:T(8,128)(2,1)S(1)}, bf16[1,128,8192]{2,1,0:T(8,128)(2,1)}, u32[]{:S(2)}) copy-start(bf16[1,128,8192]{2,1,0:T(8,128)(2,1)} %param.2) | copy-start | bytes 6291460
  37.3 39.9 %all-to-all-start.1 = ((bf16[16,24,1536]{2,1,0:T(8,128)(2,1)}), bf16[16,24,1536]{2,1,0:T(8,128)(2,1)S(1)}, u32[]{:S(2)}, u32[]{:S(2)}) async-start(bf16[16,24,1536]{2,1,0:T(8,128)(2,1)} %broadcast_in_dim.2), calls=%async_computation.1 | async-start | bytes 2359296 | tf_op jit(solution)/shard_map/all_to_all | solution.py:19
  46.7 6.7 %collective-permute-start = (bf16[24,1536]{1,0:T(8,128)(2,1)S(1)}, bf16[24,1536]{1,0:T(8,128)(2,1)S(1)}, u32[]{:S(2)}, u32[]{:S(2)}) collective-permute-start(bf16[24,1536]{1,0:T(8,128)(2,1)S(1)} %copy_bitcast_fusion), channel_id=1, source_target_pairs={{0,1},{1,0},{2,3},{3,2},{4,5},{5,4},{6,7},{7,6},{8,9},{9,8},{10,11... | collective-permute-start | bytes 221192 | tf_op jit(solution)/shard_map/ppermute | solution.py:67
  79.0 9.9 %collective-permute-start.1 = (f32[288,384]{1,0:T(8,128)S(1)}, f32[288,384]{1,0:T(8,128)S(1)}, u32[]{:S(2)}, u32[]{:S(2)}) collective-permute-start(f32[288,384]{1,0:T(8,128)S(1)} %fusion.12), channel_id=1, source_target_pairs={{0,24},{24,0},{1,25},{25,1},{2,26},{26,2},{3,27},{27,3},{4,28},{28... | collective-permute-start | bytes 1327112 | tf_op jit(solution)/shard_map/ppermute | solution.py:73
  89.9 0.9 copy-start.1
  90.8 33.3 %all-to-all-start.2 = ((bf16[12,288,128]{2,1,0:T(8,128)(2,1)}), bf16[12,288,128]{2,1,0:T(8,128)(2,1)S(1)}, u32[]{:S(2)}, u32[]{:S(2)}) async-start(bf16[12,288,128]{2,1,0:T(8,128)(2,1)} %copy-done.1), calls=%async_computation.2 | async-start | bytes 1769472 | tf_op jit(solution)/shard_map/all_to_all | solution.py:81
  124.3 7.8 %collective-permute-start.2 = (f32[144,128]{1,0:T(8,128)S(1)}, f32[144,128]{1,0:T(8,128)S(1)}, u32[]{:S(2)}, u32[]{:S(2)}) collective-permute-start(f32[144,128]{1,0:T(8,128)S(1)} %slice_select_fusion.1), channel_id=1, source_target_pairs={{0,1},{1,0},{2,3},{3,2},{4,5},{5,4},{6,7},{7,6},{8,9},{9,8},{10,11... | collective-permute-start | bytes 221192 | tf_op jit(solution)/shard_map/ppermute | solution.py:86

commit v4 on v3

--- a/solution.py
+++ b/solution.py
@@ -17,6 +17,41 @@
 def spread(part, axes):
     copies = jnp.broadcast_to(part[None], (lax.axis_size(axes),) + part.shape)
     return lax.all_to_all(copies, axes, 0, 0, tiled=True)
+
+
+def project_kernel(weight_ref, rows_ref, out_ref):
+    @pl.when(pl.program_id(0) == 0)
+    def _():
+        out_ref[...] = jnp.zeros_like(out_ref)
+
+    out_ref[...] += lax.dot_general(
+        weight_ref[...],
+        rows_ref[...],
+        (((1,), (1,)), ((), ())),
+        preferred_element_type=f32,
+    )
+
+
+def project(weight, rows, steps=8):
+    width = weight.shape[1] // steps
+    return pl.pallas_call(
+        project_kernel,
+        grid=(steps,),
+        out_shape=jax.ShapeDtypeStruct((weight.shape[0], rows.shape[0]), f32),
+        in_specs=[
+            pl.BlockSpec((weight.shape[0], width), lambda k: (0, k)),
+            pl.BlockSpec((rows.shape[0], width), lambda k: (0, k)),
+        ],
+        out_specs=pl.BlockSpec((weight.shape[0], rows.shape[0]), lambda k: (0, 0)),
+        compiler_params=pltpu.CompilerParams(vmem_limit_bytes=56 * 2**20),
+    )(weight, rows)
+
+
+def normalize(by_rows, sums, row_total):
+    feat_mean = (sums[0] / row_total)[None, :, None]
+    feat_var = (sums[1] / row_total)[None, :, None] - feat_mean * feat_mean
+    normed = ((by_rows - feat_mean) * lax.rsqrt(feat_var + epsilon)).astype(bf16)
+    return normed.transpose(1, 0, 2).reshape(by_rows.shape[1], -1)
 
 
 def product_kernel(grad_ref, other_ref, out_ref):
@@ -49,22 +84,17 @@
     feat_here = proj_weight.shape[1]
     own = feat_here // depth
     twin = lax.axis_index("twin")
-    projected = lax.dot_general(
-        proj_weight, view_rows, (((0,), (1,)), ((), ())), preferred_element_type=f32
-    )
-    projected = lax.optimization_barrier(projected)
+    projected = project(proj_weight.T, view_rows)
     by_rows = lax.all_to_all(
         projected.reshape(depth, own, rows_here), "z", 0, 0, tiled=True
     )
     sums = jnp.stack(
         [jnp.sum(by_rows, axis=(0, 2)), jnp.sum(by_rows * by_rows, axis=(0, 2))]
     )
-    sums = lax.psum(sums, "x_lo")
-    feat_mean = (sums[0] / row_total)[None, :, None]
-    feat_var = (sums[1] / row_total)[None, :, None] - feat_mean * feat_mean
-    normed = ((by_rows - feat_mean) * lax.rsqrt(feat_var + epsilon)).astype(bf16)
-    normed = normed.transpose(1, 0, 2).reshape(own, half_rows)
-    other = lax.ppermute(normed, "twin", swap)
+    normed = normalize(by_rows, lax.psum(sums, "x_lo"), row_total)
+    normed, other = lax.optimization_barrier(
+        (normed, lax.ppermute(normed, "twin", swap))
+    )
     there = spread(normed, feat_axes).reshape(feats * own, half_rows)
     here = lax.all_gather(other, "z", axis=0, tiled=True)
     corr = lax.dot_general(

time: 135 us -> 144 us (1.067)
  Pallas kernels: 0.85 us -> 8.78 us
  waiting for transfers between devices: 39 us -> 46.3 us
  matrix products: 5.51 us -> 0.63 us
  starting transfers between devices: 28 us -> 31.6 us
  local copies, waits for them, and re-layouts: 3.6 us -> 1.09 us
    all_to_all x1, waiting for transfers between devices: 0.01 us -> 7.05 us  [spread(): return lax.all_to_all(copies, axes, 0, 0, tiled=True)]
    pallas_call x0 -> x1, Pallas kernels: none -> 7 us  [project(): pl.pallas_call(project_kernel, grid=(steps,), out_shape=jax.ShapeDtypeStr...]
    ppermute x1, starting transfers between devices: 6.89 us -> 10.8 us  [shards(): take = lax.ppermute(give, 'twin', swap)]
    dot_general x1 -> x0, matrix products: 3.71 us -> none  [shards(): lax.dot_general(proj_weight, view_rows, (((0,), (1,)), ((), ())), preferr...]
    unnamed x4 -> x0, local copies, waits for them, and re-layouts: 2.5 us -> none
  transfers between devices with their start and end apart: 5 -> 5, of which waited for: 4 -> 5; matrix products, arithmetic and copies ran while one was open for 0% -> 0% of each run, Pallas kernels for 0% -> 0%
where the time goes in v4:
time: 144 us; the launch traced here: 143 us
  blocking collectives  53.2 us (37%)
  waiting for transfers between devices  46.3 us (32%)
  starting transfers between devices  31.6 us (22%)
  Pallas kernels  8.78 us (6%)
    all_to_all x1, waiting for transfers between devices, shards(): lax.all_to_all(products(grad, there, rows_here), 'z', 0, 0, tiled=True)  29 us
    all_to_all x1, blocking collectives, shards(): lax.all_to_all(projected.reshape(depth, own, rows_here), 'z', 0, 0, tiled...  27.1 us
    all_gather x1, blocking collectives, shards(): here = lax.all_gather(other, 'z', axis=0, tiled=True)  22.4 us
    ppermute x1, starting transfers between devices, shards(): take = lax.ppermute(give, 'twin', swap)  10.8 us
    all_to_all x1, starting transfers between devices, spread(): return lax.all_to_all(copies, axes, 0, 0, tiled=True)  9.39 us
    ppermute x1, waiting for transfers between devices, shards(): corr = (corr + lax.ppermute(corr, 'x_lo', swap)) / row_total  8.47 us
    all_to_all x1, waiting for transfers between devices, spread(): return lax.all_to_all(copies, axes, 0, 0, tiled=True)  7.05 us
    pallas_call x1, Pallas kernels, project(): pl.pallas_call(project_kernel, grid=(steps,), out_shape=jax.ShapeDtypeStr...  7 us
  transfers between devices with their start and end apart: 5, of which 5 were waited for; matrix products, arithmetic and copies ran while one was open for 0% of the time, Pallas kernels for 0%

profile of v4, /device:TPU:1, one launch (start us, length us, event | category | flops | bytes accessed | tf_op | source)
XLA Modules:
  0.0 143.2 jit_solution(14042785394272915240)
XLA Ops:
  0.0 7.0 %shard_map.28 = f32[288,128]{1,0:T(8,128)} custom-call(bf16[288,8192]{1,0:T(8,128)(2,1)} %bitcast.30, bf16[128,8192]{1,0:T(8,128)(2,1)} %bitcast.31), custom_call_target="tpu_custom_call" | custom-call | tf_op jit(solution)/shard_map/pallas_call | solution.py:37
  7.0 27.1 %all_to_all.15 = f32[12,24,128]{2,1,0:T(8,128)S(1)} all-to-all(f32[12,24,128]{2,1,0:T(8,128)} %bitcast.32), channel_id=1, replica_groups=mesh['x_hi'=2,'y'=8,'x_lo'=2,'z'=12,'twin'=2] {'z'}, dimensions={0} | all-to-all | bytes 294912 | tf_op jit(solution)/shard_map/all_to_all | solution.py:88
  34.1 0.1 fusion.9
  34.2 3.8 %psum.7 = f32[2,24]{1,0:T(2,128)S(1)} all-reduce(f32[2,24]{1,0:T(2,128)S(1)} %pad_maximum_fusion.1), channel_id=1, replica_groups=mesh['x_hi'=2,'y'=8,'x_lo'=2,'z'=12,'twin'=2] {'x_lo'}, use_global_device_ids=true, to_apply=%region_2.0 | all-reduce | flops 48 | bytes 384 | tf_op jit(solution)/shard_map/psum | solution.py:94
  38.0 0.1 copy_bitcast_fusion
  38.1 5.5 %collective-permute-start = (bf16[24,1536]{1,0:T(8,128)(2,1)S(1)}, bf16[24,1536]{1,0:T(8,128)(2,1)S(1)}, u32[]{:S(2)}, u32[]{:S(2)}) collective-permute-start(bf16[24,1536]{1,0:T(8,128)(2,1)S(1)} %copy_bitcast_fusion), channel_id=1, source_target_pairs={{0,1},{1,0},{2,3},{3,2},{4,5},{5,4},{6,7},{7,6},{8,9},{9,8},{10,11... | collective-permute-start | bytes 221192 | tf_op jit(solution)/shard_map/ppermute | solution.py:96
  43.6 0.9 collective-permute-done
  44.5 1.1 broadcast_in_dim.2
  45.6 9.4 %all-to-all-start.1 = ((bf16[16,24,1536]{2,1,0:T(8,128)(2,1)}), bf16[16,24,1536]{2,1,0:T(8,128)(2,1)S(1)}, u32[]{:S(2)}, u32[]{:S(2)}) async-start(bf16[16,24,1536]{2,1,0:T(8,128)(2,1)} %broadcast_in_dim.2), calls=%async_computation.1 | async-start | bytes 2359296 | tf_op jit(solution)/shard_map/all_to_all | solution.py:19
  55.0 22.4 %all_gather.3 = bf16[288,1536]{1,0:T(8,128)(2,1)S(1)} all-gather(bf16[24,1536]{1,0:T(8,128)(2,1)S(1)} %collective-permute-done), channel_id=1, replica_groups=mesh['x_hi'=2,'y'=8,'x_lo'=2,'z'=12,'twin'=2] {'z'}, dimensions={0}, use_global_device_ids=true | all-gather | bytes 958464 | tf_op jit(solution)/shard_map/all_gather | solution.py:99
  77.4 7.1 %all-to-all-done.1 = bf16[16,24,1536]{2,1,0:T(8,128)(2,1)S(1)} async-done(((bf16[16,24,1536]{2,1,0:T(8,128)(2,1)}), bf16[16,24,1536]{2,1,0:T(8,128)(2,1)S(1)}, u32[]{:S(2)}, u32[]{:S(2)}) %all-to-all-start.1) | async-done | bytes 1179680 | tf_op jit(solution)/shard_map/all_to_all | solution.py:19
  84.5 0.6 fusion.10
  85.1 2.2 %collective-permute-start.1 = (f32[288,384]{1,0:T(8,128)S(1)}, f32[288,384]{1,0:T(8,128)S(1)}, u32[]{:S(2)}, u32[]{:S(2)}) collective-permute-start(f32[288,384]{1,0:T(8,128)S(1)} %fusion.10), channel_id=1, source_target_pairs={{0,24},{24,0},{1,25},{25,1},{2,26},{26,2},{3,27},{27,3},{4,28},{28... | collective-permute-start | bytes 1327112 | tf_op jit(solution)/shard_map/ppermute | solution.py:103
  87.4 8.5 %collective-permute-done.1 = f32[288,384]{1,0:T(8,128)S(1)} collective-permute-done((f32[288,384]{1,0:T(8,128)S(1)}, f32[288,384]{1,0:T(8,128)S(1)}, u32[]{:S(2)}, u32[]{:S(2)}) %collective-permute-start.1) | collective-permute-done | bytes 442400 | tf_op jit(solution)/shard_map/ppermute | solution.py:103
  95.9 0.1 select_convert_fusion.grad_ref
  96.0 1.8 %shard_map.29 = bf16[12,288,128]{2,1,0:T(8,128)(2,1)} custom-call(bf16[288,384]{1,0:T(8,128)(2,1)S(1)} %select_convert_fusion.grad_ref, bf16[384,1536]{1,0:T(8,128)(2,1)S(1)} %bitcast.29), custom_call_target="tpu_custom_call" | custom-call | tf_op jit(solution)/shard_map/pallas_call | solution.py:69
  97.8 3.7 %all-to-all-start.2 = ((bf16[12,288,128]{2,1,0:T(8,128)(2,1)}), bf16[12,288,128]{2,1,0:T(8,128)(2,1)S(1)}, u32[]{:S(2)}, u32[]{:S(2)}) async-start(bf16[12,288,128]{2,1,0:T(8,128)(2,1)} %shard_map.29), calls=%async_computation.2 | async-start | bytes 1769472 | tf_op jit(solution)/shard_map/all_to_all | solution.py:111
  101.5 29.0 %all-to-all-done.2 = bf16[12,288,128]{2,1,0:T(8,128)(2,1)S(1)} async-done(((bf16[12,288,128]{2,1,0:T(8,128)(2,1)}), bf16[12,288,128]{2,1,0:T(8,128)(2,1)S(1)}, u32[]{:S(2)}, u32[]{:S(2)}) %all-to-all-start.2) | async-done | bytes 884768 | tf_op jit(solution)/shard_map/all_to_all | solution.py:111
  130.5 0.1 convert_reduce_fusion
  130.7 10.8 %collective-permute-start.2 = (f32[144,128]{1,0:T(8,128)S(1)}, f32[144,128]{1,0:T(8,128)S(1)}, u32[]{:S(2)}, u32[]{:S(2)}) collective-permute-start(f32[144,128]{1,0:T(8,128)S(1)} %slice_select_fusion.1), channel_id=1, source_target_pairs={{0,1},{1,0},{2,3},{3,2},{4,5},{5,4},{6,7},{7,6},{8,9},{9,8},{10,11... | collective-permute-start | bytes 221192 | tf_op jit(solution)/shard_map/ppermute | solution.py:116
  141.5 0.9 collective-permute-done.2
  142.4 0.8 pad_maximum_fusion
  (9 shorter events, 0.1 us)
Async XLA Ops:
  38.1 6.4 %collective-permute-start = (bf16[24,1536]{1,0:T(8,128)(2,1)S(1)}, bf16[24,1536]{1,0:T(8,128)(2,1)S(1)}, u32[]{:S(2)}, u32[]{:S(2)}) collective-permute-start(bf16[24,1536]{1,0:T(8,128)(2,1)S(1)} %copy_bitcast_fusion), channel_id=1, source_target_pairs={{0,1},{1,0},{2,3},{3,2},{4,5},{5,4},{6,7},{7,6},{8,9},{9,8},{10,11... | collective-permute-start | bytes 221192 | tf_op jit(solution)/shard_map/ppermute | solution.py:96
  45.6 38.9 %all-to-all-start.1 = ((bf16[16,24,1536]{2,1,0:T(8,128)(2,1)}), bf16[16,24,1536]{2,1,0:T(8,128)(2,1)S(1)}, u32[]{:S(2)}, u32[]{:S(2)}) async-start(bf16[16,24,1536]{2,1,0:T(8,128)(2,1)} %broadcast_in_dim.2), calls=%async_computation.1 | async-start | bytes 2359296 | tf_op jit(solution)/shard_map/all_to_all | solution.py:19
  85.1 10.8 %collective-permute-start.1 = (f32[288,384]{1,0:T(8,128)S(1)}, f32[288,384]{1,0:T(8,128)S(1)}, u32[]{:S(2)}, u32[]{:S(2)}) collective-permute-start(f32[288,384]{1,0:T(8,128)S(1)} %fusion.10), channel_id=1, source_target_pairs={{0,24},{24,0},{1,25},{25,1},{2,26},{26,2},{3,27},{27,3},{4,28},{28... | collective-permute-start | bytes 1327112 | tf_op jit(solution)/shard_map/ppermute | solution.py:103
  97.8 32.7 %all-to-all-start.2 = ((bf16[12,288,128]{2,1,0:T(8,128)(2,1)}), bf16[12,288,128]{2,1,0:T(8,128)(2,1)S(1)}, u32[]{:S(2)}, u32[]{:S(2)}) async-start(bf16[12,288,128]{2,1,0:T(8,128)(2,1)} %shard_map.29), calls=%async_computation.2 | async-start | bytes 1769472 | tf_op jit(solution)/shard_map/all_to_all | solution.py:111
  130.7 11.7 %collective-permute-start.2 = (f32[144,128]{1,0:T(8,128)S(1)}, f32[144,128]{1,0:T(8,128)S(1)}, u32[]{:S(2)}, u32[]{:S(2)}) collective-permute-start(f32[144,128]{1,0:T(8,128)S(1)} %slice_select_fusion.1), channel_id=1, source_target_pairs={{0,1},{1,0},{2,3},{3,2},{4,5},{5,4},{6,7},{7,6},{8,9},{9,8},{10,11... | collective-permute-start | bytes 221192 | tf_op jit(solution)/shard_map/ppermute | solution.py:116

commit v5 on v3

--- a/solution.py
+++ b/solution.py
@@ -1,3 +1,5 @@
+import functools
+
 import jax
 import jax.numpy as jnp
 from jax import lax
@@ -19,25 +21,115 @@
     return lax.all_to_all(copies, axes, 0, 0, tiled=True)
 
 
-def product_kernel(grad_ref, other_ref, out_ref):
+def project_kernel(weight_hbm, rows_hbm, out_ref, weight_ref, rows_ref, sems):
+    parts = sems.shape[1]
+    width = weight_ref.shape[1] // parts
+    copies = []
+    for part in range(parts):
+        cols = pl.ds(part * width, width)
+        pair = [
+            pltpu.make_async_copy(
+                weight_hbm.at[:, cols], weight_ref.at[:, cols], sems.at[0, part]
+            ),
+            pltpu.make_async_copy(
+                rows_hbm.at[:, cols], rows_ref.at[:, cols], sems.at[1, part]
+            ),
+        ]
+        for copy in pair:
+            copy.start()
+        copies.append(pair)
+    total = None
+    for part, pair in enumerate(copies):
+        for copy in pair:
+            copy.wait()
+        cols = slice(part * width, (part + 1) * width)
+        term = lax.dot_general(
+            weight_ref[:, cols],
+            rows_ref[:, cols],
+            (((1,), (1,)), ((), ())),
+            preferred_element_type=f32,
+        )
+        total = term if total is None else total + term
+    out_ref[...] = total
+
+
+def project(weight, rows, parts=8):
+    return pl.pallas_call(
+        project_kernel,
+        out_shape=jax.ShapeDtypeStruct((weight.shape[0], rows.shape[0]), f32),
+        in_specs=[pl.BlockSpec(memory_space=pl.ANY)] * 2,
+        out_specs=pl.BlockSpec(memory_space=pltpu.VMEM),
+        scratch_shapes=[
+            pltpu.VMEM(weight.shape, bf16),
+            pltpu.VMEM(rows.shape, bf16),
+            pltpu.SemaphoreType.DMA((2, parts)),
+        ],
+        compiler_params=pltpu.CompilerParams(vmem_limit_bytes=56 * 2**20),
+    )(weight, rows)
+
+
+def on_diagonal(place_ref, shape):
+    rows = lax.broadcasted_iota(jnp.int32, shape, 0)
+    cols = lax.broadcasted_iota(jnp.int32, shape, 1)
+    top, left, own = place_ref[0], place_ref[1], place_ref[2]
+    return (cols - rows == left - top) & (rows >= top) & (rows < top + own)
+
+
+def pack_kernel(place_ref, corr_ref, packed_ref):
+    corr = corr_ref[...]
+    feats = corr.shape[0]
+    diagonal = jnp.where(on_diagonal(place_ref, corr.shape), corr, 0.0)
+    diagonal = jnp.sum(diagonal, axis=0, keepdims=True)
+    high = diagonal.astype(bf16).astype(f32)
+    middle = (diagonal - high).astype(bf16).astype(f32)
+    low = diagonal - high - middle
+    extra = packed_ref.shape[0] - feats
+    index = lax.broadcasted_iota(jnp.int32, (extra, corr.shape[1]), 0)
+    tail = jnp.where(index == 0, high, jnp.where(index == 1, middle, low))
+    packed_ref[:feats] = corr.astype(bf16)
+    packed_ref[feats:] = jnp.where(index < 3, tail, 0.0).astype(bf16)
+
+
+def pack(place, corr):
+    return pl.pallas_call(
+        pack_kernel,
+        out_shape=jax.ShapeDtypeStruct((corr.shape[0] + 16, corr.shape[1]), bf16),
+        in_specs=[
+            pl.BlockSpec(memory_space=pltpu.SMEM),
+            pl.BlockSpec(memory_space=pltpu.VMEM),
+        ],
+        out_specs=pl.BlockSpec(memory_space=pltpu.VMEM),
+        compiler_params=pltpu.CompilerParams(vmem_limit_bytes=24 * 2**20),
+    )(place, corr)
+
+
+def product_kernel(row_total, place_ref, corr_ref, taken_ref, other_ref, out_ref):
+    feats = corr_ref.shape[0]
     rows_here = out_ref.shape[2]
+    diagonal = on_diagonal(place_ref, corr_ref.shape)
+    terms = jnp.sum(taken_ref[feats:].astype(f32), axis=0, keepdims=True)
+    taken = jnp.where(diagonal, terms, taken_ref[:feats].astype(f32))
+    corr = (corr_ref[...] + taken) / row_total
+    grad = jnp.where(diagonal, -2.0 * (1.0 - corr), 2.0 * off_weight * corr)
+    grad = grad.astype(bf16)
     for block in range(out_ref.shape[0]):
         out_ref[block] = jnp.dot(
-            grad_ref[...],
+            grad,
             other_ref[:, block * rows_here : (block + 1) * rows_here],
             preferred_element_type=f32,
         ).astype(bf16)
 
 
-def products(grad, other, rows_here):
+def products(place, corr, taken, other, rows_here, row_total):
     blocks = other.shape[1] // rows_here
     return pl.pallas_call(
-        product_kernel,
-        out_shape=jax.ShapeDtypeStruct((blocks, grad.shape[0], rows_here), bf16),
-        in_specs=[pl.BlockSpec(memory_space=pltpu.VMEM)] * 2,
+        functools.partial(product_kernel, row_total),
+        out_shape=jax.ShapeDtypeStruct((blocks, corr.shape[0], rows_here), bf16),
+        in_specs=[pl.BlockSpec(memory_space=pltpu.SMEM)]
+        + [pl.BlockSpec(memory_space=pltpu.VMEM)] * 3,
         out_specs=pl.BlockSpec(memory_space=pltpu.VMEM),
         compiler_params=pltpu.CompilerParams(vmem_limit_bytes=24 * 2**20),
-    )(grad, other)
+    )(place, corr, taken, other)
 
 
 def shards(hidden_act, proj_weight):
@@ -49,10 +141,7 @@
     feat_here = proj_weight.shape[1]
     own = feat_here // depth
     twin = lax.axis_index("twin")
-    projected = lax.dot_general(
-        proj_weight, view_rows, (((0,), (1,)), ((), ())), preferred_element_type=f32
-    )
-    projected = lax.optimization_barrier(projected)
+    projected = project(proj_weight.T, view_rows)
     by_rows = lax.all_to_all(
         projected.reshape(depth, own, rows_here), "z", 0, 0, tiled=True
     )
@@ -70,15 +159,12 @@
     corr = lax.dot_general(
         here, there, (((1,), (1,)), ((), ())), preferred_element_type=f32
     )
-    corr = (corr + lax.ppermute(corr, "x_lo", swap)) / row_total
-    row_ids = lax.broadcasted_iota(jnp.int32, corr.shape, 0)
-    row_ids = row_ids + lax.axis_index(feat_axes) * feat_here
-    cols = lax.broadcasted_iota(jnp.int32, corr.shape, 1)
-    col_ids = (cols // own) * feat_here + lax.axis_index("z") * own + cols % own
-    grad = jnp.where(
-        row_ids == col_ids, -2.0 * (1.0 - corr), 2.0 * off_weight * corr
-    ).astype(bf16)
-    terms = lax.all_to_all(products(grad, there, rows_here), "z", 0, 0, tiled=True)
+    place = jnp.stack(
+        [lax.axis_index("z") * own, lax.axis_index(feat_axes) * own, jnp.int32(own)]
+    )
+    taken = lax.ppermute(pack(place, corr), "x_lo", swap)
+    part = products(place, corr, taken, there, rows_here, row_total)
+    terms = lax.all_to_all(part, "z", 0, 0, tiled=True)
     total = jnp.sum(terms.astype(f32), axis=0)
     first, second = jnp.split(total, 2, axis=0)
     keep = jnp.where(twin == 0, first, second)

time: 135 us -> 130 us (0.963)
  Pallas kernels: 0.85 us -> 8.22 us
  waiting for transfers between devices: 39 us -> 31.7 us
  matrix products: 5.51 us -> 0.63 us
  starting transfers between devices: 28 us -> 32.1 us
  local copies, waits for them, and re-layouts: 3.6 us -> 1.08 us
    pallas_call x1 -> x3, Pallas kernels: 0.85 us -> 8.22 us  [the longest x1 5.1 us: project(): pl.pallas_call(project_kernel, out_shape=jax.ShapeDtypeStruct((weight.sha...]
    ppermute x1, starting transfers between devices: 6.89 us -> 11 us  [shards(): take = lax.ppermute(give, 'twin', swap)]
    all_to_all x1, waiting for transfers between devices: 29.6 us -> 25.5 us  [shards(): terms = lax.all_to_all(part, 'z', 0, 0, tiled=True)]
    dot_general x1 -> x0, matrix products: 3.71 us -> none  [shards(): lax.dot_general(proj_weight, view_rows, (((0,), (1,)), ((), ())), preferr...]
    ppermute x1, waiting for transfers between devices: 7.61 us -> 4.57 us  [shards(): taken = lax.ppermute(pack(place, corr), 'x_lo', swap)]
    unnamed x4 -> x0, local copies, waits for them, and re-layouts: 2.5 us -> none
where the time goes in v5:
time: 130 us; the launch traced here: 128 us
  blocking collectives  53.3 us (41%)
  starting transfers between devices  32.1 us (25%)
  waiting for transfers between devices  31.7 us (24%)
  Pallas kernels  8.22 us (6%)
    all_to_all x1, blocking collectives, shards(): lax.all_to_all(projected.reshape(depth, own, rows_here), 'z', 0, 0, tiled...  27.1 us
    all_to_all x1, waiting for transfers between devices, shards(): terms = lax.all_to_all(part, 'z', 0, 0, tiled=True)  25.5 us
    all_gather x1, blocking collectives, shards(): here = lax.all_gather(other, 'z', axis=0, tiled=True)  22.4 us
    ppermute x1, starting transfers between devices, shards(): take = lax.ppermute(give, 'twin', swap)  11 us
    all_to_all x1, starting transfers between devices, spread(): return lax.all_to_all(copies, axes, 0, 0, tiled=True)  9.39 us
    ppermute x1, starting transfers between devices, shards(): other = lax.ppermute(normed, 'twin', swap)  5.79 us
    pallas_call x1, Pallas kernels, project(): pl.pallas_call(project_kernel, out_shape=jax.ShapeDtypeStruct((weight.sha...  5.1 us
    ppermute x1, waiting for transfers between devices, shards(): taken = lax.ppermute(pack(place, corr), 'x_lo', swap)  4.57 us
  transfers between devices with their start and end apart: 5, of which 4 were waited for; matrix products, arithmetic and copies ran while one was open for 0% of the time, Pallas kernels for 0%

profile of v5, /device:TPU:1, one launch (start us, length us, event | category | flops | bytes accessed | tf_op | source)
XLA Modules:
  0.0 128.5 jit_solution(12657642494387128326)
XLA Ops:
  0.0 5.1 %shard_map.28 = f32[288,128]{1,0:T(8,128)} custom-call(bf16[288,8192]{1,0:T(8,128)(2,1)} %bitcast.32, bf16[128,8192]{1,0:T(8,128)(2,1)} %bitcast.33), custom_call_target="tpu_custom_call" | custom-call | tf_op jit(solution)/shard_map/pallas_call | solution.py:57
  5.1 27.1 %all_to_all.15 = f32[12,24,128]{2,1,0:T(8,128)S(1)} all-to-all(f32[12,24,128]{2,1,0:T(8,128)} %bitcast.34), channel_id=1, replica_groups=mesh['x_hi'=2,'y'=8,'x_lo'=2,'z'=12,'twin'=2] {'z'}, dimensions={0} | all-to-all | bytes 294912 | tf_op jit(solution)/shard_map/all_to_all | solution.py:145
  32.2 0.1 fusion.3
  32.3 3.8 %psum.7 = f32[2,24]{1,0:T(2,128)S(1)} all-reduce(f32[2,24]{1,0:T(2,128)S(1)} %pad_maximum_fusion.1), channel_id=1, replica_groups=mesh['x_hi'=2,'y'=8,'x_lo'=2,'z'=12,'twin'=2] {'x_lo'}, use_global_device_ids=true, to_apply=%region_2.0 | all-reduce | flops 48 | bytes 384 | tf_op jit(solution)/shard_map/psum | solution.py:151
  36.1 0.1 copy_bitcast_fusion
  36.2 1.1 broadcast_in_dim.2
  37.3 9.4 %all-to-all-start.1 = ((bf16[16,24,1536]{2,1,0:T(8,128)(2,1)}), bf16[16,24,1536]{2,1,0:T(8,128)(2,1)S(1)}, u32[]{:S(2)}, u32[]{:S(2)}) async-start(bf16[16,24,1536]{2,1,0:T(8,128)(2,1)} %broadcast_in_dim.2), calls=%async_computation.1 | async-start | bytes 2359296 | tf_op jit(solution)/shard_map/all_to_all | solution.py:21
  46.7 5.8 %collective-permute-start = (bf16[24,1536]{1,0:T(8,128)(2,1)S(1)}, bf16[24,1536]{1,0:T(8,128)(2,1)S(1)}, u32[]{:S(2)}, u32[]{:S(2)}) collective-permute-start(bf16[24,1536]{1,0:T(8,128)(2,1)S(1)} %copy_bitcast_fusion), channel_id=1, source_target_pairs={{0,1},{1,0},{2,3},{3,2},{4,5},{5,4},{6,7},{7,6},{8,9},{9,8},{10,11... | collective-permute-start | bytes 221192 | tf_op jit(solution)/shard_map/ppermute | solution.py:156
  52.5 0.1 pad_add_fusion.place_ref
  52.6 0.8 collective-permute-done
  53.4 22.4 %all_gather.3 = bf16[288,1536]{1,0:T(8,128)(2,1)S(1)} all-gather(bf16[24,1536]{1,0:T(8,128)(2,1)S(1)} %collective-permute-done), channel_id=1, replica_groups=mesh['x_hi'=2,'y'=8,'x_lo'=2,'z'=12,'twin'=2] {'z'}, dimensions={0}, use_global_device_ids=true | all-gather | bytes 958464 | tf_op jit(solution)/shard_map/all_gather | solution.py:158
  75.9 0.0 all-to-all-done.1
  75.9 0.6 fusion.4.corr_ref
  76.5 0.7 shard_map.29
  77.2 2.2 %collective-permute-start.1 = (bf16[304,384]{1,0:T(8,128)(2,1)S(1)}, bf16[304,384]{1,0:T(8,128)(2,1)S(1)}, u32[]{:S(2)}, u32[]{:S(2)}) collective-permute-start(bf16[304,384]{1,0:T(8,128)(2,1)S(1)} %shard_map.29), channel_id=1, source_target_pairs={{0,24},{24,0},{1,25},{25,1},{2,26},{26,2},{3,27},{27,3},{4,28},{28... | collective-permute-start | bytes 700424 | tf_op jit(solution)/shard_map/ppermute | solution.py:165
  79.4 4.6 %collective-permute-done.1.taken_ref = bf16[304,384]{1,0:T(8,128)(2,1)S(1)} collective-permute-done((bf16[304,384]{1,0:T(8,128)(2,1)S(1)}, bf16[304,384]{1,0:T(8,128)(2,1)S(1)}, u32[]{:S(2)}, u32[]{:S(2)}) %collective-permute-start.1) | collective-permute-done | bytes 233504 | tf_op jit(solution)/shard_map/ppermute | solution.py:165
  84.0 2.4 %shard_map.30 = bf16[12,288,128]{2,1,0:T(8,128)(2,1)} custom-call(s32[3]{0:T(128)S(1)} %pad_add_fusion.place_ref, f32[288,384]{1,0:T(8,128)S(1)} %fusion.4.corr_ref, bf16[304,384]{1,0:T(8,128)(2,1)S(1)} %collective-permute-done.1.taken_ref, bf16[384,1536]{1,0:T(8,128)(2,1)S(1)} %bitcast.31), custom_call_target="tpu_custom_call" | custom-call | tf_op jit(solution)/shard_map/pallas_call | solution.py:125
  86.4 3.7 %all-to-all-start.2 = ((bf16[12,288,128]{2,1,0:T(8,128)(2,1)}), bf16[12,288,128]{2,1,0:T(8,128)(2,1)S(1)}, u32[]{:S(2)}, u32[]{:S(2)}) async-start(bf16[12,288,128]{2,1,0:T(8,128)(2,1)} %shard_map.30), calls=%async_computation.2 | async-start | bytes 1769472 | tf_op jit(solution)/shard_map/all_to_all | solution.py:167
  90.1 25.5 %all-to-all-done.2 = bf16[12,288,128]{2,1,0:T(8,128)(2,1)S(1)} async-done(((bf16[12,288,128]{2,1,0:T(8,128)(2,1)}), bf16[12,288,128]{2,1,0:T(8,128)(2,1)S(1)}, u32[]{:S(2)}, u32[]{:S(2)}) %all-to-all-start.2) | async-done | bytes 884768 | tf_op jit(solution)/shard_map/all_to_all | solution.py:167
  115.6 0.1 convert_reduce_fusion
  115.7 11.0 %collective-permute-start.2 = (f32[144,128]{1,0:T(8,128)S(1)}, f32[144,128]{1,0:T(8,128)S(1)}, u32[]{:S(2)}, u32[]{:S(2)}) collective-permute-start(f32[144,128]{1,0:T(8,128)S(1)} %slice_select_fusion.1), channel_id=1, source_target_pairs={{0,1},{1,0},{2,3},{3,2},{4,5},{5,4},{6,7},{7,6},{8,9},{9,8},{10,11... | collective-permute-start | bytes 221192 | tf_op jit(solution)/shard_map/ppermute | solution.py:172
  126.8 0.9 collective-permute-done.2
  127.7 0.8 pad_maximum_fusion
  (5 shorter events, 0.1 us)
Async XLA Ops:
  37.3 38.5 %all-to-all-start.1 = ((bf16[16,24,1536]{2,1,0:T(8,128)(2,1)}), bf16[16,24,1536]{2,1,0:T(8,128)(2,1)S(1)}, u32[]{:S(2)}, u32[]{:S(2)}) async-start(bf16[16,24,1536]{2,1,0:T(8,128)(2,1)} %broadcast_in_dim.2), calls=%async_computation.1 | async-start | bytes 2359296 | tf_op jit(solution)/shard_map/all_to_all | solution.py:21
  46.7 6.7 %collective-permute-start = (bf16[24,1536]{1,0:T(8,128)(2,1)S(1)}, bf16[24,1536]{1,0:T(8,128)(2,1)S(1)}, u32[]{:S(2)}, u32[]{:S(2)}) collective-permute-start(bf16[24,1536]{1,0:T(8,128)(2,1)S(1)} %copy_bitcast_fusion), channel_id=1, source_target_pairs={{0,1},{1,0},{2,3},{3,2},{4,5},{5,4},{6,7},{7,6},{8,9},{9,8},{10,11... | collective-permute-start | bytes 221192 | tf_op jit(solution)/shard_map/ppermute | solution.py:156
  77.2 6.8 %collective-permute-start.1 = (bf16[304,384]{1,0:T(8,128)(2,1)S(1)}, bf16[304,384]{1,0:T(8,128)(2,1)S(1)}, u32[]{:S(2)}, u32[]{:S(2)}) collective-permute-start(bf16[304,384]{1,0:T(8,128)(2,1)S(1)} %shard_map.29), channel_id=1, source_target_pairs={{0,24},{24,0},{1,25},{25,1},{2,26},{26,2},{3,27},{27,3},{4,28},{28... | collective-permute-start | bytes 700424 | tf_op jit(solution)/shard_map/ppermute | solution.py:165
  86.4 29.2 %all-to-all-start.2 = ((bf16[12,288,128]{2,1,0:T(8,128)(2,1)}), bf16[12,288,128]{2,1,0:T(8,128)(2,1)S(1)}, u32[]{:S(2)}, u32[]{:S(2)}) async-start(bf16[12,288,128]{2,1,0:T(8,128)(2,1)} %shard_map.30), calls=%async_computation.2 | async-start | bytes 1769472 | tf_op jit(solution)/shard_map/all_to_all | solution.py:167
  115.7 11.9 %collective-permute-start.2 = (f32[144,128]{1,0:T(8,128)S(1)}, f32[144,128]{1,0:T(8,128)S(1)}, u32[]{:S(2)}, u32[]{:S(2)}) collective-permute-start(f32[144,128]{1,0:T(8,128)S(1)} %slice_select_fusion.1), channel_id=1, source_target_pairs={{0,1},{1,0},{2,3},{3,2},{4,5},{5,4},{6,7},{7,6},{8,9},{9,8},{10,11... | collective-permute-start | bytes 221192 | tf_op jit(solution)/shard_map/ppermute | solution.py:172

commit v6 on v5

--- a/solution.py
+++ b/solution.py
@@ -153,14 +153,19 @@
     feat_var = (sums[1] / row_total)[None, :, None] - feat_mean * feat_mean
     normed = ((by_rows - feat_mean) * lax.rsqrt(feat_var + epsilon)).astype(bf16)
     normed = normed.transpose(1, 0, 2).reshape(own, half_rows)
+    far = lax.ppermute(normed, "x_hi", swap)
     other = lax.ppermute(normed, "twin", swap)
-    there = spread(normed, feat_axes).reshape(feats * own, half_rows)
+    low = lax.axis_index("x_hi") == 0
+    pair = jnp.concatenate([jnp.where(low, normed, far), jnp.where(low, far, normed)])
+    pair, other = lax.optimization_barrier((pair, other))
+    there = spread(pair, "y").reshape(feats * own, half_rows)
     here = lax.all_gather(other, "z", axis=0, tiled=True)
     corr = lax.dot_general(
         here, there, (((1,), (1,)), ((), ())), preferred_element_type=f32
     )
+    chunk = lax.axis_index("y") * lax.axis_size("x_hi") + lax.axis_index("x_hi")
     place = jnp.stack(
-        [lax.axis_index("z") * own, lax.axis_index(feat_axes) * own, jnp.int32(own)]
+        [lax.axis_index("z") * own, chunk * own, jnp.int32(own)]
     )
     taken = lax.ppermute(pack(place, corr), "x_lo", swap)
     part = products(place, corr, taken, there, rows_here, row_total)

time: 130 us -> 146 us (1.12)
  waiting for transfers between devices: 31.7 us -> 48.4 us
    all_to_all x1, waiting for transfers between devices: 0.01 us -> 9.77 us  [spread(): return lax.all_to_all(copies, axes, 0, 0, tiled=True)]
    all_to_all x1, waiting for transfers between devices: 25.5 us -> 30.5 us  [shards(): terms = lax.all_to_all(part, 'z', 0, 0, tiled=True)]
    ppermute x0 -> x1, starting transfers between devices: none -> 4.65 us  [shards(): far = lax.ppermute(normed, 'x_hi', swap)]
    all_to_all x1, starting transfers between devices: 9.39 us -> 6.82 us  [spread(): return lax.all_to_all(copies, axes, 0, 0, tiled=True)]
    ppermute x1, waiting for transfers between devices: 4.57 us -> 6.52 us  [shards(): taken = lax.ppermute(pack(place, corr), 'x_lo', swap)]
    ppermute x1, starting transfers between devices: 11 us -> 9.37 us  [shards(): take = lax.ppermute(give, 'twin', swap)]
  transfers between devices with their start and end apart: 5 -> 6, of which waited for: 4 -> 5; matrix products, arithmetic and copies ran while one was open for 0% -> 0% of each run, Pallas kernels for 0% -> 0%
where the time goes in v6:
time: 146 us; the launch traced here: 145 us
  blocking collectives  53.1 us (36%)
  waiting for transfers between devices  48.4 us (33%)
  starting transfers between devices  32.5 us (22%)
  Pallas kernels  8.21 us (6%)
    all_to_all x1, waiting for transfers between devices, shards(): terms = lax.all_to_all(part, 'z', 0, 0, tiled=True)  30.5 us
    all_to_all x1, blocking collectives, shards(): lax.all_to_all(projected.reshape(depth, own, rows_here), 'z', 0, 0, tiled...  27.1 us
    all_gather x1, blocking collectives, shards(): here = lax.all_gather(other, 'z', axis=0, tiled=True)  22.2 us
    all_to_all x1, waiting for transfers between devices, spread(): return lax.all_to_all(copies, axes, 0, 0, tiled=True)  9.77 us
    ppermute x1, starting transfers between devices, shards(): take = lax.ppermute(give, 'twin', swap)  9.37 us
    all_to_all x1, starting transfers between devices, spread(): return lax.all_to_all(copies, axes, 0, 0, tiled=True)  6.82 us
    ppermute x1, waiting for transfers between devices, shards(): taken = lax.ppermute(pack(place, corr), 'x_lo', swap)  6.52 us
    ppermute x1, starting transfers between devices, shards(): other = lax.ppermute(normed, 'twin', swap)  5.79 us
  transfers between devices with their start and end apart: 6, of which 5 were waited for; matrix products, arithmetic and copies ran while one was open for 0% of the time, Pallas kernels for 0%

profile of v6, /device:TPU:1, one launch (start us, length us, event | category | flops | bytes accessed | tf_op | source)
XLA Modules:
  0.0 145.4 jit_solution(1422283644415496337)
XLA Ops:
  0.0 5.1 %shard_map.28 = f32[288,128]{1,0:T(8,128)} custom-call(bf16[288,8192]{1,0:T(8,128)(2,1)} %bitcast.37, bf16[128,8192]{1,0:T(8,128)(2,1)} %bitcast.38), custom_call_target="tpu_custom_call" | custom-call | tf_op jit(solution)/shard_map/pallas_call | solution.py:57
  5.1 27.1 %all_to_all.15 = f32[12,24,128]{2,1,0:T(8,128)S(1)} all-to-all(f32[12,24,128]{2,1,0:T(8,128)} %bitcast.39), channel_id=1, replica_groups=mesh['x_hi'=2,'y'=8,'x_lo'=2,'z'=12,'twin'=2] {'z'}, dimensions={0} | all-to-all | bytes 294912 | tf_op jit(solution)/shard_map/all_to_all | solution.py:145
  32.2 0.1 fusion.3
  32.3 3.8 %psum.7 = f32[2,24]{1,0:T(2,128)S(1)} all-reduce(f32[2,24]{1,0:T(2,128)S(1)} %pad_maximum_fusion.2), channel_id=1, replica_groups=mesh['x_hi'=2,'y'=8,'x_lo'=2,'z'=12,'twin'=2] {'x_lo'}, use_global_device_ids=true, to_apply=%region_2.0 | all-reduce | flops 48 | bytes 384 | tf_op jit(solution)/shard_map/psum | solution.py:151
  36.1 0.1 copy_bitcast_fusion
  36.2 4.7 %collective-permute-start = (bf16[24,1536]{1,0:T(8,128)(2,1)S(1)}, bf16[24,1536]{1,0:T(8,128)(2,1)S(1)}, u32[]{:S(2)}, u32[]{:S(2)}) collective-permute-start(bf16[24,1536]{1,0:T(8,128)(2,1)S(1)} %copy_bitcast_fusion), channel_id=1, source_target_pairs={{0,384},{384,0},{1,385},{385,1},{2,386},{386,2},{3,387},{387,3},{4... | collective-permute-start | bytes 221192 | tf_op jit(solution)/shard_map/ppermute | solution.py:156
  40.9 5.8 %collective-permute-start.1 = (bf16[24,1536]{1,0:T(8,128)(2,1)S(1)}, bf16[24,1536]{1,0:T(8,128)(2,1)S(1)}, u32[]{:S(2)}, u32[]{:S(2)}) collective-permute-start(bf16[24,1536]{1,0:T(8,128)(2,1)S(1)} %copy_bitcast_fusion), channel_id=1, source_target_pairs={{0,1},{1,0},{2,3},{3,2},{4,5},{5,4},{6,7},{7,6},{8,9},{9,8},{10,11... | collective-permute-start | bytes 221192 | tf_op jit(solution)/shard_map/ppermute | solution.py:157
  46.7 0.1 broadcast_select_fusion.1
  46.8 0.8 collective-permute-done.1
  47.6 1.1 broadcast_in_dim.2
  48.7 6.8 %all-to-all-start.1 = ((bf16[8,48,1536]{2,1,0:T(8,128)(2,1)}), bf16[8,48,1536]{2,1,0:T(8,128)(2,1)S(1)}, u32[]{:S(2)}, u32[]{:S(2)}) async-start(bf16[8,48,1536]{2,1,0:T(8,128)(2,1)} %broadcast_in_dim.2), calls=%async_computation.1 | async-start | bytes 2359296 | tf_op jit(solution)/shard_map/all_to_all | solution.py:21
  55.6 22.2 %all_gather.3 = bf16[288,1536]{1,0:T(8,128)(2,1)S(1)} all-gather(bf16[24,1536]{1,0:T(8,128)(2,1)S(1)} %collective-permute-done.1), channel_id=1, replica_groups=mesh['x_hi'=2,'y'=8,'x_lo'=2,'z'=12,'twin'=2] {'z'}, dimensions={0}, use_global_device_ids=true | all-gather | bytes 958464 | tf_op jit(solution)/shard_map/all_gather | solution.py:162
  77.8 9.8 %all-to-all-done.1 = bf16[8,48,1536]{2,1,0:T(8,128)(2,1)S(1)} async-done(((bf16[8,48,1536]{2,1,0:T(8,128)(2,1)}), bf16[8,48,1536]{2,1,0:T(8,128)(2,1)S(1)}, u32[]{:S(2)}, u32[]{:S(2)}) %all-to-all-start.1) | async-done | bytes 1179680 | tf_op jit(solution)/shard_map/all_to_all | solution.py:21
  87.6 0.6 fusion.4.corr_ref
  88.2 0.7 shard_map.29
  88.9 2.1 %collective-permute-start.2 = (bf16[304,384]{1,0:T(8,128)(2,1)S(1)}, bf16[304,384]{1,0:T(8,128)(2,1)S(1)}, u32[]{:S(2)}, u32[]{:S(2)}) collective-permute-start(bf16[304,384]{1,0:T(8,128)(2,1)S(1)} %shard_map.29), channel_id=1, source_target_pairs={{0,24},{24,0},{1,25},{25,1},{2,26},{26,2},{3,27},{27,3},{4,28},{28... | collective-permute-start | bytes 700424 | tf_op jit(solution)/shard_map/ppermute | solution.py:170
  91.1 6.5 %collective-permute-done.2.taken_ref = bf16[304,384]{1,0:T(8,128)(2,1)S(1)} collective-permute-done((bf16[304,384]{1,0:T(8,128)(2,1)S(1)}, bf16[304,384]{1,0:T(8,128)(2,1)S(1)}, u32[]{:S(2)}, u32[]{:S(2)}) %collective-permute-start.2) | collective-permute-done | bytes 233504 | tf_op jit(solution)/shard_map/ppermute | solution.py:170
  97.6 2.4 %shard_map.30 = bf16[12,288,128]{2,1,0:T(8,128)(2,1)} custom-call(s32[3]{0:T(128)S(1)} %pad_add_fusion.place_ref, f32[288,384]{1,0:T(8,128)S(1)} %fusion.4.corr_ref, bf16[304,384]{1,0:T(8,128)(2,1)S(1)} %collective-permute-done.2.taken_ref, bf16[384,1536]{1,0:T(8,128)(2,1)S(1)} %bitcast.36), custom_call_target="tpu_custom_call" | custom-call | tf_op jit(solution)/shard_map/pallas_call | solution.py:125
  100.0 3.7 %all-to-all-start.2 = ((bf16[12,288,128]{2,1,0:T(8,128)(2,1)}), bf16[12,288,128]{2,1,0:T(8,128)(2,1)S(1)}, u32[]{:S(2)}, u32[]{:S(2)}) async-start(bf16[12,288,128]{2,1,0:T(8,128)(2,1)} %shard_map.30), calls=%async_computation.2 | async-start | bytes 1769472 | tf_op jit(solution)/shard_map/all_to_all | solution.py:172
  103.7 30.5 %all-to-all-done.2 = bf16[12,288,128]{2,1,0:T(8,128)(2,1)S(1)} async-done(((bf16[12,288,128]{2,1,0:T(8,128)(2,1)}), bf16[12,288,128]{2,1,0:T(8,128)(2,1)S(1)}, u32[]{:S(2)}, u32[]{:S(2)}) %all-to-all-start.2) | async-done | bytes 884768 | tf_op jit(solution)/shard_map/all_to_all | solution.py:172
  134.2 0.1 convert_reduce_fusion
  134.3 9.4 %collective-permute-start.3 = (f32[144,128]{1,0:T(8,128)S(1)}, f32[144,128]{1,0:T(8,128)S(1)}, u32[]{:S(2)}, u32[]{:S(2)}) collective-permute-start(f32[144,128]{1,0:T(8,128)S(1)} %slice_select_fusion.1), channel_id=1, source_target_pairs={{0,1},{1,0},{2,3},{3,2},{4,5},{5,4},{6,7},{7,6},{8,9},{9,8},{10,11... | collective-permute-start | bytes 221192 | tf_op jit(solution)/shard_map/ppermute | solution.py:177
  143.7 0.9 collective-permute-done.3
  144.6 0.8 pad_maximum_fusion.1
  (8 shorter events, 0.1 us)
Async XLA Ops:
  36.2 10.5 %collective-permute-start = (bf16[24,1536]{1,0:T(8,128)(2,1)S(1)}, bf16[24,1536]{1,0:T(8,128)(2,1)S(1)}, u32[]{:S(2)}, u32[]{:S(2)}) collective-permute-start(bf16[24,1536]{1,0:T(8,128)(2,1)S(1)} %copy_bitcast_fusion), channel_id=1, source_target_pairs={{0,384},{384,0},{1,385},{385,1},{2,386},{386,2},{3,387},{387,3},{4... | collective-permute-start | bytes 221192 | tf_op jit(solution)/shard_map/ppermute | solution.py:156
  40.9 6.7 %collective-permute-start.1 = (bf16[24,1536]{1,0:T(8,128)(2,1)S(1)}, bf16[24,1536]{1,0:T(8,128)(2,1)S(1)}, u32[]{:S(2)}, u32[]{:S(2)}) collective-permute-start(bf16[24,1536]{1,0:T(8,128)(2,1)S(1)} %copy_bitcast_fusion), channel_id=1, source_target_pairs={{0,1},{1,0},{2,3},{3,2},{4,5},{5,4},{6,7},{7,6},{8,9},{9,8},{10,11... | collective-permute-start | bytes 221192 | tf_op jit(solution)/shard_map/ppermute | solution.py:157
  48.7 38.9 %all-to-all-start.1 = ((bf16[8,48,1536]{2,1,0:T(8,128)(2,1)}), bf16[8,48,1536]{2,1,0:T(8,128)(2,1)S(1)}, u32[]{:S(2)}, u32[]{:S(2)}) async-start(bf16[8,48,1536]{2,1,0:T(8,128)(2,1)} %broadcast_in_dim.2), calls=%async_computation.1 | async-start | bytes 2359296 | tf_op jit(solution)/shard_map/all_to_all | solution.py:21
  88.9 8.7 %collective-permute-start.2 = (bf16[304,384]{1,0:T(8,128)(2,1)S(1)}, bf16[304,384]{1,0:T(8,128)(2,1)S(1)}, u32[]{:S(2)}, u32[]{:S(2)}) collective-permute-start(bf16[304,384]{1,0:T(8,128)(2,1)S(1)} %shard_map.29), channel_id=1, source_target_pairs={{0,24},{24,0},{1,25},{25,1},{2,26},{26,2},{3,27},{27,3},{4,28},{28... | collective-permute-start | bytes 700424 | tf_op jit(solution)/shard_map/ppermute | solution.py:170
  100.0 34.2 %all-to-all-start.2 = ((bf16[12,288,128]{2,1,0:T(8,128)(2,1)}), bf16[12,288,128]{2,1,0:T(8,128)(2,1)S(1)}, u32[]{:S(2)}, u32[]{:S(2)}) async-start(bf16[12,288,128]{2,1,0:T(8,128)(2,1)} %shard_map.30), calls=%async_computation.2 | async-start | bytes 1769472 | tf_op jit(solution)/shard_map/all_to_all | solution.py:172
  134.3 10.3 %collective-permute-start.3 = (f32[144,128]{1,0:T(8,128)S(1)}, f32[144,128]{1,0:T(8,128)S(1)}, u32[]{:S(2)}, u32[]{:S(2)}) collective-permute-start(f32[144,128]{1,0:T(8,128)S(1)} %slice_select_fusion.1), channel_id=1, source_target_pairs={{0,1},{1,0},{2,3},{3,2},{4,5},{5,4},{6,7},{7,6},{8,9},{9,8},{10,11... | collective-permute-start | bytes 221192 | tf_op jit(solution)/shard_map/ppermute | solution.py:177

commit v7 on v5

--- a/solution.py
+++ b/solution.py
@@ -19,6 +19,12 @@
 def spread(part, axes):
     copies = jnp.broadcast_to(part[None], (lax.axis_size(axes),) + part.shape)
     return lax.all_to_all(copies, axes, 0, 0, tiled=True)
+
+
+def trade(part):
+    both = lax.all_gather(part, "twin", axis=0, tiled=True)
+    first, second = jnp.split(both, 2, axis=0)
+    return jnp.where(lax.axis_index("twin") == 0, second, first)
 
 
 def project_kernel(weight_hbm, rows_hbm, out_ref, weight_ref, rows_ref, sems):
@@ -148,12 +154,12 @@
     sums = jnp.stack(
         [jnp.sum(by_rows, axis=(0, 2)), jnp.sum(by_rows * by_rows, axis=(0, 2))]
     )
-    sums = lax.psum(sums, "x_lo")
+    sums = jnp.sum(lax.all_gather(sums, "x_lo", axis=0), axis=0)
     feat_mean = (sums[0] / row_total)[None, :, None]
     feat_var = (sums[1] / row_total)[None, :, None] - feat_mean * feat_mean
     normed = ((by_rows - feat_mean) * lax.rsqrt(feat_var + epsilon)).astype(bf16)
     normed = normed.transpose(1, 0, 2).reshape(own, half_rows)
-    other = lax.ppermute(normed, "twin", swap)
+    other = trade(normed)
     there = spread(normed, feat_axes).reshape(feats * own, half_rows)
     here = lax.all_gather(other, "z", axis=0, tiled=True)
     corr = lax.dot_general(
@@ -169,7 +175,7 @@
     first, second = jnp.split(total, 2, axis=0)
     keep = jnp.where(twin == 0, first, second)
     give = jnp.where(twin == 0, second, first)
-    take = lax.ppermute(give, "twin", swap)
+    take = trade(give)
     return jnp.stack(
         [jnp.where(twin == 0, take, keep), jnp.where(twin == 0, keep, take)], axis=1
     )

time: 130 us -> 127 us (0.977); the launches traced: 128 us -> 127 us
  blocking collectives: 53.3 us -> 100 us
  waiting for transfers between devices: 31.7 us -> 4.58 us
  starting transfers between devices: 32.1 us -> 11.6 us
    all_to_all x0 -> x1, blocking collectives: none -> 31.5 us  [shards(): terms = lax.all_to_all(part, 'z', 0, 0, tiled=True)]
    all_to_all x1 -> x0, waiting for transfers between devices: 25.5 us -> none  [shards(): terms = lax.all_to_all(part, 'z', 0, 0, tiled=True)]
    all_gather x0 -> x3, blocking collectives: none -> 19.2 us  [the longest x2 16.1 us: trade(): both = lax.all_gather(part, 'twin', axis=0, tiled=True)]
    ppermute x2 -> x0, starting transfers between devices: 16.8 us -> none  [the longest x1 11 us: shards(): take = lax.ppermute(give, 'twin', swap)]
    psum x1 -> x0, blocking collectives: 3.8 us -> none  [shards(): sums = lax.psum(sums, 'x_lo')]
    all_to_all x1 -> x0, starting transfers between devices: 3.69 us -> none  [shards(): terms = lax.all_to_all(part, 'z', 0, 0, tiled=True)]
    ppermute x2 -> x0, waiting for transfers between devices: 1.7 us -> none  [the longest x1 0.89 us: shards(): take = lax.ppermute(give, 'twin', swap)]
  transfers between devices with their start and end apart: 5 -> 2, of which waited for: 4 -> 1; matrix products, arithmetic and copies ran while one was open for 0% -> 0% of each run, Pallas kernels for 0% -> 0%
where the time goes in v7:
time: 127 us
  blocking collectives  100 us (79%)
  starting transfers between devices  11.6 us (9%)
  Pallas kernels  7.28 us (6%)
  waiting for transfers between devices  4.58 us (4%)
  other arithmetic  1.28 us (1%)
    all_to_all x1, blocking collectives, shards(): terms = lax.all_to_all(part, 'z', 0, 0, tiled=True)  31.5 us
    all_to_all x1, blocking collectives, shards(): lax.all_to_all(projected.reshape(depth, own, rows_here), 'z', 0, 0, tiled...  27.1 us
    all_gather x1, blocking collectives, shards(): here = lax.all_gather(other, 'z', axis=0, tiled=True)  22.7 us
    all_gather x2, blocking collectives, trade(): both = lax.all_gather(part, 'twin', axis=0, tiled=True)  16.1 us
    all_to_all x1, starting transfers between devices, spread(): return lax.all_to_all(copies, axes, 0, 0, tiled=True)  9.39 us
    pallas_call x1, Pallas kernels, project(): pl.pallas_call(project_kernel, out_shape=jax.ShapeDtypeStruct((weight.sha...  5.1 us
    ppermute x1, waiting for transfers between devices, shards(): taken = lax.ppermute(pack(place, corr), 'x_lo', swap)  4.58 us
    all_gather x1, blocking collectives, shards(): sums = jnp.sum(lax.all_gather(sums, 'x_lo', axis=0), axis=0)  3.1 us
  transfers between devices with their start and end apart: 2, of which 1 were waited for; matrix products, arithmetic and copies ran while one was open for 0% of the time, Pallas kernels for 0%

profile of v7, /device:TPU:1, one launch (start us, length us, event | category | flops | bytes accessed | tf_op | source)
XLA Modules:
  0.0 127.0 jit_solution(9939846793625991422)
XLA Ops:
  0.0 5.1 %shard_map.28 = f32[288,128]{1,0:T(8,128)} custom-call(bf16[288,8192]{1,0:T(8,128)(2,1)} %bitcast.34, bf16[128,8192]{1,0:T(8,128)(2,1)} %bitcast.35), custom_call_target="tpu_custom_call" | custom-call | tf_op jit(solution)/shard_map/pallas_call | solution.py:63
  5.1 27.1 %all_to_all.15 = f32[12,24,128]{2,1,0:T(8,128)S(1)} all-to-all(f32[12,24,128]{2,1,0:T(8,128)} %bitcast.36), channel_id=1, replica_groups=mesh['x_hi'=2,'y'=8,'x_lo'=2,'z'=12,'twin'=2] {'z'}, dimensions={0} | all-to-all | bytes 294912 | tf_op jit(solution)/shard_map/all_to_all | solution.py:151
  32.2 0.1 fusion.3
  32.3 3.1 %all-gather.1 = f32[2,2,24]{2,1,0:T(2,128)S(1)} all-gather(f32[1,2,24]{2,1,0:T(2,128)S(1)} %maximum_bitcast_fusion), channel_id=2, replica_groups=mesh['x_hi'=2,'y'=8,'x_lo'=2,'z'=12,'twin'=2] {'x_lo'}, dimensions={0}, use_global_device_ids=true | all-gather | bytes 576 | tf_op jit(solution)/shard_map/all_gather | solution.py:157
  35.4 0.1 copy_bitcast_fusion
  35.5 1.1 broadcast_in_dim.2
  36.6 9.4 %all-to-all-start.1 = ((bf16[16,24,1536]{2,1,0:T(8,128)(2,1)}), bf16[16,24,1536]{2,1,0:T(8,128)(2,1)S(1)}, u32[]{:S(2)}, u32[]{:S(2)}) async-start(bf16[16,24,1536]{2,1,0:T(8,128)(2,1)} %broadcast_in_dim.2), calls=%async_computation.1 | async-start | bytes 2359296 | tf_op jit(solution)/shard_map/all_to_all | solution.py:21
  46.0 0.1 pad_add_fusion.place_ref
  46.1 5.4 %all_gather.17 = bf16[48,1536]{1,0:T(8,128)(2,1)S(1)} all-gather(bf16[24,1536]{1,0:T(8,128)(2,1)S(1)} %copy_bitcast_fusion), channel_id=1, replica_groups=mesh['x_hi'=2,'y'=8,'x_lo'=2,'z'=12,'twin'=2] {'twin'}, dimensions={0}, use_global_device_ids=true | all-gather | bytes 221184 | tf_op jit(solution)/shard_map/all_gather | solution.py:25
  51.6 22.7 %all_gather.18 = bf16[288,1536]{1,0:T(8,128)(2,1)S(1)} all-gather(bf16[24,1536]{1,0:T(8,128)(2,1)S(1)} %slice_select_fusion.1), channel_id=1, replica_groups=mesh['x_hi'=2,'y'=8,'x_lo'=2,'z'=12,'twin'=2] {'z'}, dimensions={0}, use_global_device_ids=true | all-gather | bytes 958464 | tf_op jit(solution)/shard_map/all_gather | solution.py:164
  74.2 0.0 all-to-all-done.1
  74.2 0.6 fusion.4.corr_ref
  74.9 0.7 shard_map.29
  75.6 2.2 %collective-permute-start = (bf16[304,384]{1,0:T(8,128)(2,1)S(1)}, bf16[304,384]{1,0:T(8,128)(2,1)S(1)}, u32[]{:S(2)}, u32[]{:S(2)}) collective-permute-start(bf16[304,384]{1,0:T(8,128)(2,1)S(1)} %shard_map.29), channel_id=1, source_target_pairs={{0,24},{24,0},{1,25},{25,1},{2,26},{26,2},{3,27},{27,3},{4,28},{28... | collective-permute-start | bytes 700424 | tf_op jit(solution)/shard_map/ppermute | solution.py:171
  77.8 4.6 %collective-permute-done.taken_ref = bf16[304,384]{1,0:T(8,128)(2,1)S(1)} collective-permute-done((bf16[304,384]{1,0:T(8,128)(2,1)S(1)}, bf16[304,384]{1,0:T(8,128)(2,1)S(1)}, u32[]{:S(2)}, u32[]{:S(2)}) %collective-permute-start) | collective-permute-done | bytes 233504 | tf_op jit(solution)/shard_map/ppermute | solution.py:171
  82.4 1.5 %shard_map.30 = bf16[12,288,128]{2,1,0:T(8,128)(2,1)S(1)} custom-call(s32[3]{0:T(128)S(1)} %pad_add_fusion.place_ref, f32[288,384]{1,0:T(8,128)S(1)} %fusion.4.corr_ref, bf16[304,384]{1,0:T(8,128)(2,1)S(1)} %collective-permute-done.taken_ref, bf16[384,1536]{1,0:T(8,128)(2,1)S(1)} %bitcast.33), custom_call_target="tpu_custom_call" | custom-call | tf_op jit(solution)/shard_map/pallas_call | solution.py:131
  83.9 31.5 %all_to_all.16 = bf16[12,288,128]{2,1,0:T(8,128)(2,1)S(1)} all-to-all(bf16[12,288,128]{2,1,0:T(8,128)(2,1)S(1)} %shard_map.30), channel_id=1, replica_groups=mesh['x_hi'=2,'y'=8,'x_lo'=2,'z'=12,'twin'=2] {'z'}, dimensions={0} | all-to-all | bytes 1769472 | tf_op jit(solution)/shard_map/all_to_all | solution.py:173
  115.3 0.1 convert_reduce_fusion
  115.5 10.7 %all_gather.19 = f32[288,128]{1,0:T(8,128)S(1)} all-gather(f32[144,128]{1,0:T(8,128)S(1)} %slice_select_fusion.3), channel_id=1, replica_groups=mesh['x_hi'=2,'y'=8,'x_lo'=2,'z'=12,'twin'=2] {'twin'}, dimensions={0}, use_global_device_ids=true | all-gather | bytes 221184 | tf_op jit(solution)/shard_map/all_gather | solution.py:25
  126.2 0.8 pad_maximum_fusion
  (7 shorter events, 0.1 us)
Async XLA Ops:
  36.6 37.6 %all-to-all-start.1 = ((bf16[16,24,1536]{2,1,0:T(8,128)(2,1)}), bf16[16,24,1536]{2,1,0:T(8,128)(2,1)S(1)}, u32[]{:S(2)}, u32[]{:S(2)}) async-start(bf16[16,24,1536]{2,1,0:T(8,128)(2,1)} %broadcast_in_dim.2), calls=%async_computation.1 | async-start | bytes 2359296 | tf_op jit(solution)/shard_map/all_to_all | solution.py:21
  75.6 6.8 %collective-permute-start = (bf16[304,384]{1,0:T(8,128)(2,1)S(1)}, bf16[304,384]{1,0:T(8,128)(2,1)S(1)}, u32[]{:S(2)}, u32[]{:S(2)}) collective-permute-start(bf16[304,384]{1,0:T(8,128)(2,1)S(1)} %shard_map.29), channel_id=1, source_target_pairs={{0,24},{24,0},{1,25},{25,1},{2,26},{26,2},{3,27},{27,3},{4,28},{28... | collective-permute-start | bytes 700424 | tf_op jit(solution)/shard_map/ppermute | solution.py:171

commit v8 on v7

--- a/solution.py
+++ b/solution.py
@@ -10,7 +10,8 @@
 
 epsilon = 1e-05
 off_weight = 0.0051
-batch_axes = ("x_lo", "z")
+depth_axes = ("z_hi", "z_lo")
+batch_axes = ("x_lo",) + depth_axes
 feat_axes = ("x_hi", "y")
 bf16, f32 = jnp.bfloat16, jnp.float32
 swap = [(0, 1), (1, 0)]
@@ -109,7 +110,9 @@
     )(place, corr)
 
 
-def product_kernel(row_total, place_ref, corr_ref, taken_ref, other_ref, out_ref):
+def product_kernel(
+    row_total, near_count, place_ref, corr_ref, taken_ref, other_ref, out_ref
+):
     feats = corr_ref.shape[0]
     rows_here = out_ref.shape[2]
     diagonal = on_diagonal(place_ref, corr_ref.shape)
@@ -118,18 +121,20 @@
     corr = (corr_ref[...] + taken) / row_total
     grad = jnp.where(diagonal, -2.0 * (1.0 - corr), 2.0 * off_weight * corr)
     grad = grad.astype(bf16)
-    for block in range(out_ref.shape[0]):
-        out_ref[block] = jnp.dot(
+    blocks = out_ref.shape[0]
+    for block in range(blocks):
+        far, near = divmod(block, near_count)
+        out_ref[near * (blocks // near_count) + far] = jnp.dot(
             grad,
             other_ref[:, block * rows_here : (block + 1) * rows_here],
             preferred_element_type=f32,
         ).astype(bf16)
 
 
-def products(place, corr, taken, other, rows_here, row_total):
+def products(place, corr, taken, other, rows_here, row_total, near_count):
     blocks = other.shape[1] // rows_here
     return pl.pallas_call(
-        functools.partial(product_kernel, row_total),
+        functools.partial(product_kernel, row_total, near_count),
         out_shape=jax.ShapeDtypeStruct((blocks, corr.shape[0], rows_here), bf16),
         in_specs=[pl.BlockSpec(memory_space=pltpu.SMEM)]
         + [pl.BlockSpec(memory_space=pltpu.VMEM)] * 3,
@@ -139,7 +144,7 @@
 
 
 def shards(hidden_act, proj_weight):
-    depth, feats = lax.axis_size("z"), lax.axis_size(feat_axes)
+    depth, feats = lax.axis_size(depth_axes), lax.axis_size(feat_axes)
     view_rows = hidden_act[0]
     rows_here = view_rows.shape[0]
     half_rows = rows_here * depth
@@ -149,7 +154,7 @@
     twin = lax.axis_index("twin")
     projected = project(proj_weight.T, view_rows)
     by_rows = lax.all_to_all(
-        projected.reshape(depth, own, rows_here), "z", 0, 0, tiled=True
+        projected.reshape(depth, own, rows_here), depth_axes, 0, 0, tiled=True
     )
     sums = jnp.stack(
         [jnp.sum(by_rows, axis=(0, 2)), jnp.sum(by_rows * by_rows, axis=(0, 2))]
@@ -161,16 +166,20 @@
     normed = normed.transpose(1, 0, 2).reshape(own, half_rows)
     other = trade(normed)
     there = spread(normed, feat_axes).reshape(feats * own, half_rows)
-    here = lax.all_gather(other, "z", axis=0, tiled=True)
+    here = lax.all_gather(other, depth_axes, axis=0, tiled=True)
     corr = lax.dot_general(
         here, there, (((1,), (1,)), ((), ())), preferred_element_type=f32
     )
     place = jnp.stack(
-        [lax.axis_index("z") * own, lax.axis_index(feat_axes) * own, jnp.int32(own)]
+        [lax.axis_index(depth_axes) * own, lax.axis_index(feat_axes) * own, jnp.int32(own)]
     )
     taken = lax.ppermute(pack(place, corr), "x_lo", swap)
-    part = products(place, corr, taken, there, rows_here, row_total)
-    terms = lax.all_to_all(part, "z", 0, 0, tiled=True)
+    near_count = lax.axis_size("z_lo")
+    part = products(place, corr, taken, there, rows_here, row_total, near_count)
+    terms = lax.all_to_all(part, "z_lo", 0, 0, tiled=True)
+    near = terms.reshape((near_count, -1) + terms.shape[1:]).astype(f32)
+    near = jnp.sum(near, axis=0).astype(bf16)
+    terms = lax.all_to_all(near, "z_hi", 0, 0, tiled=True)
     total = jnp.sum(terms.astype(f32), axis=0)
     first, second = jnp.split(total, 2, axis=0)
     keep = jnp.where(twin == 0, first, second)
@@ -184,11 +193,13 @@
 def solution(mesh):
     parts = 2
     shape = mesh.devices.shape
+    depth = shape[1] // parts
+    near = 3 if depth % 3 == 0 else 1
     fine = Mesh(
         mesh.devices.reshape(
-            parts, shape[0] // parts, parts, shape[1] // parts, shape[2]
+            parts, shape[0] // parts, parts, depth // near, near, shape[2]
         ),
-        ("x_hi", "y", "x_lo", "z", "twin"),
+        ("x_hi", "y", "x_lo", "z_hi", "z_lo", "twin"),
     )
     return jax.shard_map(
         shards,

time: 127 us -> 124 us (0.976)
  blocking collectives: 100 us -> 97.2 us
    all_to_all x2 -> x3, blocking collectives: 58.5 us -> 55.1 us  [the longest x1 27.1 us: shards(): lax.all_to_all(projected.reshape(depth, own, rows_here), depth_axes, 0, 0...]
where the time goes in v8:
time: 124 us
  blocking collectives  97.2 us (78%)
  starting transfers between devices  11.6 us (9%)
  Pallas kernels  7.28 us (6%)
  waiting for transfers between devices  4.58 us (4%)
  local copies, waits for them, and re-layouts  1.82 us (1%)
    all_to_all x1, blocking collectives, shards(): lax.all_to_all(projected.reshape(depth, own, rows_here), depth_axes, 0, 0...  27.1 us
    all_gather x1, blocking collectives, shards(): here = lax.all_gather(other, depth_axes, axis=0, tiled=True)  22.7 us
    all_gather x2, blocking collectives, trade(): both = lax.all_gather(part, 'twin', axis=0, tiled=True)  16.3 us
    all_to_all x1, blocking collectives, shards(): terms = lax.all_to_all(near, 'z_hi', 0, 0, tiled=True)  16.1 us
    all_to_all x1, blocking collectives, shards(): terms = lax.all_to_all(part, 'z_lo', 0, 0, tiled=True)  11.9 us
    all_to_all x1, starting transfers between devices, spread(): return lax.all_to_all(copies, axes, 0, 0, tiled=True)  9.39 us
    pallas_call x1, Pallas kernels, project(): pl.pallas_call(project_kernel, out_shape=jax.ShapeDtypeStruct((weight.sha...  5.1 us
    ppermute x1, waiting for transfers between devices, shards(): taken = lax.ppermute(pack(place, corr), 'x_lo', swap)  4.58 us
  transfers between devices with their start and end apart: 2, of which 1 were waited for; matrix products, arithmetic and copies ran while one was open for 0% of the time, Pallas kernels for 0%

profile of v8, /device:TPU:1, one launch (start us, length us, event | category | flops | bytes accessed | tf_op | source)
XLA Modules:
  0.0 123.9 jit_solution(9903924988750453153)
XLA Ops:
  0.0 5.1 %shard_map.28 = f32[288,128]{1,0:T(8,128)} custom-call(bf16[288,8192]{1,0:T(8,128)(2,1)} %bitcast.35, bf16[128,8192]{1,0:T(8,128)(2,1)} %bitcast.37), custom_call_target="tpu_custom_call" | custom-call | tf_op jit(solution)/shard_map/pallas_call | solution.py:64
  5.1 27.1 %all_to_all.20 = f32[12,24,128]{2,1,0:T(8,128)S(1)} all-to-all(f32[12,24,128]{2,1,0:T(8,128)} %bitcast.38), channel_id=1, replica_groups=mesh['x_hi'=2,'y'=8,'x_lo'=2,'z_hi'=4,'z_lo'=3,'twin'=2] {'z_hi','z_lo'}, dimensions={0} | all-to-all | bytes 294912 | tf_op jit(solution)/shard_map/all_to_all | solution.py:156
  32.2 0.1 fusion.3
  32.3 3.1 %all-gather.1 = f32[2,2,24]{2,1,0:T(2,128)S(1)} all-gather(f32[1,2,24]{2,1,0:T(2,128)S(1)} %maximum_bitcast_fusion), channel_id=2, replica_groups=mesh['x_hi'=2,'y'=8,'x_lo'=2,'z_hi'=4,'z_lo'=3,'twin'=2] {'x_lo'}, dimensions={0}, use_global_device_ids=true | all-gather | bytes 576 | tf_op jit(solution)/shard_map/all_gather | solution.py:162
  35.4 0.1 copy_bitcast_fusion
  35.5 1.1 broadcast_in_dim.2
  36.6 9.4 %all-to-all-start.1 = ((bf16[16,24,1536]{2,1,0:T(8,128)(2,1)}), bf16[16,24,1536]{2,1,0:T(8,128)(2,1)S(1)}, u32[]{:S(2)}, u32[]{:S(2)}) async-start(bf16[16,24,1536]{2,1,0:T(8,128)(2,1)} %broadcast_in_dim.2), calls=%async_computation.1 | async-start | bytes 2359296 | tf_op jit(solution)/shard_map/all_to_all | solution.py:22
  46.0 0.1 pad_add_fusion.place_ref
  46.1 5.4 %all_gather.17 = bf16[48,1536]{1,0:T(8,128)(2,1)S(1)} all-gather(bf16[24,1536]{1,0:T(8,128)(2,1)S(1)} %copy_bitcast_fusion), channel_id=1, replica_groups=mesh['x_hi'=2,'y'=8,'x_lo'=2,'z_hi'=4,'z_lo'=3,'twin'=2] {'twin'}, dimensions={0}, use_global_device_ids=true | all-gather | bytes 221184 | tf_op jit(solution)/shard_map/all_gather | solution.py:26
  51.6 22.7 %all_gather.18 = bf16[288,1536]{1,0:T(8,128)(2,1)S(1)} all-gather(bf16[24,1536]{1,0:T(8,128)(2,1)S(1)} %slice_select_fusion.1), channel_id=1, replica_groups=mesh['x_hi'=2,'y'=8,'x_lo'=2,'z_hi'=4,'z_lo'=3,'twin'=2] {'z_hi','z_lo'}, dimensions={0}, use_global_device_ids=true | all-gather | bytes 958464 | tf_op jit(solution)/shard_map/all_gather | solution.py:169
  74.2 0.0 all-to-all-done.1
  74.3 0.6 fusion.4.corr_ref
  74.9 0.7 shard_map.29
  75.6 2.2 %collective-permute-start = (bf16[304,384]{1,0:T(8,128)(2,1)S(1)}, bf16[304,384]{1,0:T(8,128)(2,1)S(1)}, u32[]{:S(2)}, u32[]{:S(2)}) collective-permute-start(bf16[304,384]{1,0:T(8,128)(2,1)S(1)} %shard_map.29), channel_id=1, source_target_pairs={{0,24},{24,0},{1,25},{25,1},{2,26},{26,2},{3,27},{27,3},{4,28},{28... | collective-permute-start | bytes 700424 | tf_op jit(solution)/shard_map/ppermute | solution.py:176
  77.8 4.6 %collective-permute-done.taken_ref = bf16[304,384]{1,0:T(8,128)(2,1)S(1)} collective-permute-done((bf16[304,384]{1,0:T(8,128)(2,1)S(1)}, bf16[304,384]{1,0:T(8,128)(2,1)S(1)}, u32[]{:S(2)}, u32[]{:S(2)}) %collective-permute-start) | collective-permute-done | bytes 233504 | tf_op jit(solution)/shard_map/ppermute | solution.py:176
  82.4 1.5 %shard_map.30 = bf16[12,288,128]{2,1,0:T(8,128)(2,1)S(1)} custom-call(s32[3]{0:T(128)S(1)} %pad_add_fusion.place_ref, f32[288,384]{1,0:T(8,128)S(1)} %fusion.4.corr_ref, bf16[304,384]{1,0:T(8,128)(2,1)S(1)} %collective-permute-done.taken_ref, bf16[384,1536]{1,0:T(8,128)(2,1)S(1)} %bitcast.34), custom_call_target="tpu_custom_call" | custom-call | tf_op jit(solution)/shard_map/pallas_call | solution.py:136
  83.9 11.9 %all_to_all.21 = bf16[12,288,128]{2,1,0:T(8,128)(2,1)S(1)} all-to-all(bf16[12,288,128]{2,1,0:T(8,128)(2,1)S(1)} %shard_map.30), channel_id=1, replica_groups=mesh['x_hi'=2,'y'=8,'x_lo'=2,'z_hi'=4,'z_lo'=3,'twin'=2] {'z_lo'}, dimensions={0} | all-to-all | bytes 1769472 | tf_op jit(solution)/shard_map/all_to_all | solution.py:179
  95.8 0.2 reduce_sum.51
  96.1 16.1 %all_to_all.22 = bf16[4,288,128]{2,1,0:T(8,128)(2,1)S(1)} all-to-all(bf16[4,288,128]{2,1,0:T(8,128)(2,1)S(1)} %reduce_sum.51), channel_id=1, replica_groups=mesh['x_hi'=2,'y'=8,'x_lo'=2,'z_hi'=4,'z_lo'=3,'twin'=2] {'z_hi'}, dimensions={0} | all-to-all | bytes 589824 | tf_op jit(solution)/shard_map/all_to_all | solution.py:182
  112.2 10.9 %all_gather.19 = f32[288,128]{1,0:T(8,128)S(1)} all-gather(f32[144,128]{1,0:T(8,128)S(1)} %slice_select_fusion.3), channel_id=1, replica_groups=mesh['x_hi'=2,'y'=8,'x_lo'=2,'z_hi'=4,'z_lo'=3,'twin'=2] {'twin'}, dimensions={0}, use_global_device_ids=true | all-gather | bytes 221184 | tf_op jit(solution)/shard_map/all_gather | solution.py:26
  123.2 0.7 copy.9
  (9 shorter events, 0.1 us)
Async XLA Ops:
  36.6 37.6 %all-to-all-start.1 = ((bf16[16,24,1536]{2,1,0:T(8,128)(2,1)}), bf16[16,24,1536]{2,1,0:T(8,128)(2,1)S(1)}, u32[]{:S(2)}, u32[]{:S(2)}) async-start(bf16[16,24,1536]{2,1,0:T(8,128)(2,1)} %broadcast_in_dim.2), calls=%async_computation.1 | async-start | bytes 2359296 | tf_op jit(solution)/shard_map/all_to_all | solution.py:22
  75.6 6.8 %collective-permute-start = (bf16[304,384]{1,0:T(8,128)(2,1)S(1)}, bf16[304,384]{1,0:T(8,128)(2,1)S(1)}, u32[]{:S(2)}, u32[]{:S(2)}) collective-permute-start(bf16[304,384]{1,0:T(8,128)(2,1)S(1)} %shard_map.29), channel_id=1, source_target_pairs={{0,24},{24,0},{1,25},{25,1},{2,26},{26,2},{3,27},{27,3},{4,28},{28... | collective-permute-start | bytes 700424 | tf_op jit(solution)/shard_map/ppermute | solution.py:176

commit v9 on v8

--- a/solution.py
+++ b/solution.py
@@ -153,9 +153,11 @@
     own = feat_here // depth
     twin = lax.axis_index("twin")
     projected = project(proj_weight.T, view_rows)
-    by_rows = lax.all_to_all(
-        projected.reshape(depth, own, rows_here), depth_axes, 0, 0, tiled=True
-    )
+    near_count = lax.axis_size("z_lo")
+    by_rows = projected.reshape(-1, near_count, own, rows_here)
+    by_rows = lax.all_to_all(by_rows, "z_lo", 1, 1, tiled=True)
+    by_rows = lax.all_to_all(by_rows, "z_hi", 0, 0, tiled=True)
+    by_rows = by_rows.reshape(depth, own, rows_here)
     sums = jnp.stack(
         [jnp.sum(by_rows, axis=(0, 2)), jnp.sum(by_rows * by_rows, axis=(0, 2))]
     )
@@ -174,7 +176,6 @@
         [lax.axis_index(depth_axes) * own, lax.axis_index(feat_axes) * own, jnp.int32(own)]
     )
     taken = lax.ppermute(pack(place, corr), "x_lo", swap)
-    near_count = lax.axis_size("z_lo")
     part = products(place, corr, taken, there, rows_here, row_total, near_count)
     terms = lax.all_to_all(part, "z_lo", 0, 0, tiled=True)
     near = terms.reshape((near_count, -1) + terms.shape[1:]).astype(f32)

time: 124 us -> 132 us (1.065)
  blocking collectives: 97.2 us -> 104 us
    all_to_all x1 -> x2, blocking collectives: 27.1 us -> 34.4 us  [the longest x1 24.2 us: shards(): by_rows = lax.all_to_all(by_rows, 'z_hi', 0, 0, tiled=True)]
where the time goes in v9:
time: 132 us
  blocking collectives  104 us (79%)
  starting transfers between devices  11.6 us (9%)
  Pallas kernels  7.28 us (6%)
  waiting for transfers between devices  4.59 us (3%)
  local copies, waits for them, and re-layouts  2.76 us (2%)
    all_to_all x1, blocking collectives, shards(): by_rows = lax.all_to_all(by_rows, 'z_hi', 0, 0, tiled=True)  24.2 us
    all_gather x1, blocking collectives, shards(): here = lax.all_gather(other, depth_axes, axis=0, tiled=True)  22.5 us
    all_gather x2, blocking collectives, trade(): both = lax.all_gather(part, 'twin', axis=0, tiled=True)  16.5 us
    all_to_all x1, blocking collectives, shards(): terms = lax.all_to_all(near, 'z_hi', 0, 0, tiled=True)  15.1 us
    all_to_all x1, blocking collectives, shards(): terms = lax.all_to_all(part, 'z_lo', 0, 0, tiled=True)  12.4 us
    all_to_all x1, blocking collectives, shards(): by_rows = lax.all_to_all(by_rows, 'z_lo', 1, 1, tiled=True)  10.2 us
    all_to_all x1, starting transfers between devices, spread(): return lax.all_to_all(copies, axes, 0, 0, tiled=True)  9.38 us
    pallas_call x1, Pallas kernels, project(): pl.pallas_call(project_kernel, out_shape=jax.ShapeDtypeStruct((weight.sha...  5.1 us
  transfers between devices with their start and end apart: 2, of which 1 were waited for; matrix products, arithmetic and copies ran while one was open for 0% of the time, Pallas kernels for 0%

profile of v9, /device:TPU:1, one launch (start us, length us, event | category | flops | bytes accessed | tf_op | source)
XLA Modules:
  0.0 131.7 jit_solution(3212121116698331384)
XLA Ops:
  0.0 5.1 %shard_map.28 = f32[288,128]{1,0:T(8,128)} custom-call(bf16[288,8192]{1,0:T(8,128)(2,1)} %bitcast.41, bf16[128,8192]{1,0:T(8,128)(2,1)} %bitcast.43), custom_call_target="tpu_custom_call" | custom-call | tf_op jit(solution)/shard_map/pallas_call | solution.py:64
  5.1 0.9 copy.13
  6.0 10.2 %all_to_all.25 = f32[4,3,24,128]{3,2,0,1:T(8,128)S(1)} all-to-all(f32[4,3,24,128]{3,2,0,1:T(8,128)S(1)} %copy.13), channel_id=1, replica_groups=mesh['x_hi'=2,'y'=8,'x_lo'=2,'z_hi'=4,'z_lo'=3,'twin'=2] {'z_lo'}, dimensions={1} | all-to-all | bytes 294912 | tf_op jit(solution)/shard_map/all_to_all | solution.py:158
  16.2 24.2 %all_to_all.26 = f32[4,3,24,128]{3,2,1,0:T(8,128)S(1)} all-to-all(f32[4,3,24,128]{3,2,1,0:T(8,128)S(1)} %copy.14), channel_id=1, replica_groups=mesh['x_hi'=2,'y'=8,'x_lo'=2,'z_hi'=4,'z_lo'=3,'twin'=2] {'z_hi'}, dimensions={0} | all-to-all | bytes 294912 | tf_op jit(solution)/shard_map/all_to_all | solution.py:159
  40.4 0.1 fusion.4
  40.6 3.1 %all-gather.1 = f32[2,2,24]{2,1,0:T(2,128)S(1)} all-gather(f32[1,2,24]{2,1,0:T(2,128)S(1)} %maximum_bitcast_fusion), channel_id=2, replica_groups=mesh['x_hi'=2,'y'=8,'x_lo'=2,'z_hi'=4,'z_lo'=3,'twin'=2] {'x_lo'}, dimensions={0}, use_global_device_ids=true | all-gather | bytes 576 | tf_op jit(solution)/shard_map/all_gather | solution.py:164
  43.7 0.1 fusion.1
  43.8 1.1 broadcast_in_dim.2
  44.9 9.4 %all-to-all-start.2 = ((bf16[16,24,1536]{2,1,0:T(8,128)(2,1)}), bf16[16,24,1536]{2,1,0:T(8,128)(2,1)S(1)}, u32[]{:S(2)}, u32[]{:S(2)}) async-start(bf16[16,24,1536]{2,1,0:T(8,128)(2,1)} %broadcast_in_dim.2), calls=%async_computation.2 | async-start | bytes 2359296 | tf_op jit(solution)/shard_map/all_to_all | solution.py:22
  54.3 0.1 pad_add_fusion.place_ref
  54.4 6.1 %all_gather.17 = bf16[48,1536]{1,0:T(8,128)(2,1)S(1)} all-gather(bf16[24,1536]{1,0:T(8,128)(2,1)S(1)} %copy_bitcast_fusion), channel_id=1, replica_groups=mesh['x_hi'=2,'y'=8,'x_lo'=2,'z_hi'=4,'z_lo'=3,'twin'=2] {'twin'}, dimensions={0}, use_global_device_ids=true | all-gather | bytes 221184 | tf_op jit(solution)/shard_map/all_gather | solution.py:26
  60.5 22.5 %all_gather.18 = bf16[288,1536]{1,0:T(8,128)(2,1)S(1)} all-gather(bf16[24,1536]{1,0:T(8,128)(2,1)S(1)} %slice_select_fusion.1), channel_id=1, replica_groups=mesh['x_hi'=2,'y'=8,'x_lo'=2,'z_hi'=4,'z_lo'=3,'twin'=2] {'z_hi','z_lo'}, dimensions={0}, use_global_device_ids=true | all-gather | bytes 958464 | tf_op jit(solution)/shard_map/all_gather | solution.py:171
  83.0 0.0 all-to-all-done.2
  83.0 0.6 fusion.5.corr_ref
  83.6 0.7 shard_map.29
  84.3 2.2 %collective-permute-start = (bf16[304,384]{1,0:T(8,128)(2,1)S(1)}, bf16[304,384]{1,0:T(8,128)(2,1)S(1)}, u32[]{:S(2)}, u32[]{:S(2)}) collective-permute-start(bf16[304,384]{1,0:T(8,128)(2,1)S(1)} %shard_map.29), channel_id=1, source_target_pairs={{0,24},{24,0},{1,25},{25,1},{2,26},{26,2},{3,27},{27,3},{4,28},{28... | collective-permute-start | bytes 700424 | tf_op jit(solution)/shard_map/ppermute | solution.py:178
  86.5 4.6 %collective-permute-done.taken_ref = bf16[304,384]{1,0:T(8,128)(2,1)S(1)} collective-permute-done((bf16[304,384]{1,0:T(8,128)(2,1)S(1)}, bf16[304,384]{1,0:T(8,128)(2,1)S(1)}, u32[]{:S(2)}, u32[]{:S(2)}) %collective-permute-start) | collective-permute-done | bytes 233504 | tf_op jit(solution)/shard_map/ppermute | solution.py:178
  91.1 1.5 %shard_map.30 = bf16[12,288,128]{2,1,0:T(8,128)(2,1)S(1)} custom-call(s32[3]{0:T(128)S(1)} %pad_add_fusion.place_ref, f32[288,384]{1,0:T(8,128)S(1)} %fusion.5.corr_ref, bf16[304,384]{1,0:T(8,128)(2,1)S(1)} %collective-permute-done.taken_ref, bf16[384,1536]{1,0:T(8,128)(2,1)S(1)} %bitcast.40), custom_call_target="tpu_custom_call" | custom-call | tf_op jit(solution)/shard_map/pallas_call | solution.py:136
  92.6 12.4 %all_to_all.27 = bf16[12,288,128]{2,1,0:T(8,128)(2,1)S(1)} all-to-all(bf16[12,288,128]{2,1,0:T(8,128)(2,1)S(1)} %shard_map.30), channel_id=1, replica_groups=mesh['x_hi'=2,'y'=8,'x_lo'=2,'z_hi'=4,'z_lo'=3,'twin'=2] {'z_lo'}, dimensions={0} | all-to-all | bytes 1769472 | tf_op jit(solution)/shard_map/all_to_all | solution.py:180
  105.1 0.2 reduce_sum.51
  105.3 15.1 %all_to_all.28 = bf16[4,288,128]{2,1,0:T(8,128)(2,1)S(1)} all-to-all(bf16[4,288,128]{2,1,0:T(8,128)(2,1)S(1)} %reduce_sum.51), channel_id=1, replica_groups=mesh['x_hi'=2,'y'=8,'x_lo'=2,'z_hi'=4,'z_lo'=3,'twin'=2] {'z_hi'}, dimensions={0} | all-to-all | bytes 589824 | tf_op jit(solution)/shard_map/all_to_all | solution.py:183
  120.5 10.4 %all_gather.19 = f32[288,128]{1,0:T(8,128)S(1)} all-gather(f32[144,128]{1,0:T(8,128)S(1)} %slice_select_fusion.3), channel_id=1, replica_groups=mesh['x_hi'=2,'y'=8,'x_lo'=2,'z_hi'=4,'z_lo'=3,'twin'=2] {'twin'}, dimensions={0}, use_global_device_ids=true | all-gather | bytes 221184 | tf_op jit(solution)/shard_map/all_gather | solution.py:26
  131.0 0.7 copy.16
  (11 shorter events, 0.1 us)
Async XLA Ops:
  44.9 38.1 %all-to-all-start.2 = ((bf16[16,24,1536]{2,1,0:T(8,128)(2,1)}), bf16[16,24,1536]{2,1,0:T(8,128)(2,1)S(1)}, u32[]{:S(2)}, u32[]{:S(2)}) async-start(bf16[16,24,1536]{2,1,0:T(8,128)(2,1)} %broadcast_in_dim.2), calls=%async_computation.2 | async-start | bytes 2359296 | tf_op jit(solution)/shard_map/all_to_all | solution.py:22
  84.3 6.8 %collective-permute-start = (bf16[304,384]{1,0:T(8,128)(2,1)S(1)}, bf16[304,384]{1,0:T(8,128)(2,1)S(1)}, u32[]{:S(2)}, u32[]{:S(2)}) collective-permute-start(bf16[304,384]{1,0:T(8,128)(2,1)S(1)} %shard_map.29), channel_id=1, source_target_pairs={{0,24},{24,0},{1,25},{25,1},{2,26},{26,2},{3,27},{27,3},{4,28},{28... | collective-permute-start | bytes 700424 | tf_op jit(solution)/shard_map/ppermute | solution.py:178

commit v10 on v8

--- a/solution.py
+++ b/solution.py
@@ -194,7 +194,7 @@
     parts = 2
     shape = mesh.devices.shape
     depth = shape[1] // parts
-    near = 3 if depth % 3 == 0 else 1
+    near = 4 if depth % 4 == 0 else 1
     fine = Mesh(
         mesh.devices.reshape(
             parts, shape[0] // parts, parts, depth // near, near, shape[2]

time: 124 us -> 126 us (1.016)
  blocking collectives: 97.2 us -> 99.3 us
    all_to_all x1, blocking collectives: 11.9 us -> 21.9 us  [shards(): terms = lax.all_to_all(part, 'z_lo', 0, 0, tiled=True)]
    all_gather x2, blocking collectives: 16.3 us -> 12.4 us  [trade(): both = lax.all_gather(part, 'twin', axis=0, tiled=True)]
    all_to_all x1, blocking collectives: 16.1 us -> 12.2 us  [shards(): terms = lax.all_to_all(near, 'z_hi', 0, 0, tiled=True)]
where the time goes in v10:
time: 126 us
  blocking collectives  99.3 us (79%)
  starting transfers between devices  11.6 us (9%)
  Pallas kernels  7.28 us (6%)
  waiting for transfers between devices  4.59 us (4%)
  local copies, waits for them, and re-layouts  1.82 us (1%)
    all_to_all x1, blocking collectives, shards(): lax.all_to_all(projected.reshape(depth, own, rows_here), depth_axes, 0, 0...  27.1 us
    all_gather x1, blocking collectives, shards(): here = lax.all_gather(other, depth_axes, axis=0, tiled=True)  22.7 us
    all_to_all x1, blocking collectives, shards(): terms = lax.all_to_all(part, 'z_lo', 0, 0, tiled=True)  21.9 us
    all_gather x2, blocking collectives, trade(): both = lax.all_gather(part, 'twin', axis=0, tiled=True)  12.4 us
    all_to_all x1, blocking collectives, shards(): terms = lax.all_to_all(near, 'z_hi', 0, 0, tiled=True)  12.2 us
    all_to_all x1, starting transfers between devices, spread(): return lax.all_to_all(copies, axes, 0, 0, tiled=True)  9.39 us
    pallas_call x1, Pallas kernels, project(): pl.pallas_call(project_kernel, out_shape=jax.ShapeDtypeStruct((weight.sha...  5.1 us
    ppermute x1, waiting for transfers between devices, shards(): taken = lax.ppermute(pack(place, corr), 'x_lo', swap)  4.59 us
  transfers between devices with their start and end apart: 2, of which 1 were waited for; matrix products, arithmetic and copies ran while one was open for 0% of the time, Pallas kernels for 0%

profile of v10, /device:TPU:1, one launch (start us, length us, event | category | flops | bytes accessed | tf_op | source)
XLA Modules:
  0.0 125.9 jit_solution(5347760922992715776)
XLA Ops:
  0.0 5.1 %shard_map.28 = f32[288,128]{1,0:T(8,128)} custom-call(bf16[288,8192]{1,0:T(8,128)(2,1)} %bitcast.35, bf16[128,8192]{1,0:T(8,128)(2,1)} %bitcast.37), custom_call_target="tpu_custom_call" | custom-call | tf_op jit(solution)/shard_map/pallas_call | solution.py:64
  5.1 27.1 %all_to_all.20 = f32[12,24,128]{2,1,0:T(8,128)S(1)} all-to-all(f32[12,24,128]{2,1,0:T(8,128)} %bitcast.38), channel_id=1, replica_groups=mesh['x_hi'=2,'y'=8,'x_lo'=2,'z_hi'=3,'z_lo'=4,'twin'=2] {'z_hi','z_lo'}, dimensions={0} | all-to-all | bytes 294912 | tf_op jit(solution)/shard_map/all_to_all | solution.py:156
  32.2 0.1 fusion.3
  32.3 3.1 %all-gather.1 = f32[2,2,24]{2,1,0:T(2,128)S(1)} all-gather(f32[1,2,24]{2,1,0:T(2,128)S(1)} %maximum_bitcast_fusion), channel_id=2, replica_groups=mesh['x_hi'=2,'y'=8,'x_lo'=2,'z_hi'=3,'z_lo'=4,'twin'=2] {'x_lo'}, dimensions={0}, use_global_device_ids=true | all-gather | bytes 576 | tf_op jit(solution)/shard_map/all_gather | solution.py:162
  35.4 0.1 copy_bitcast_fusion
  35.5 1.1 broadcast_in_dim.2
  36.6 9.4 %all-to-all-start.1 = ((bf16[16,24,1536]{2,1,0:T(8,128)(2,1)}), bf16[16,24,1536]{2,1,0:T(8,128)(2,1)S(1)}, u32[]{:S(2)}, u32[]{:S(2)}) async-start(bf16[16,24,1536]{2,1,0:T(8,128)(2,1)} %broadcast_in_dim.2), calls=%async_computation.1 | async-start | bytes 2359296 | tf_op jit(solution)/shard_map/all_to_all | solution.py:22
  46.0 0.1 pad_add_fusion.place_ref
  46.1 5.4 %all_gather.17 = bf16[48,1536]{1,0:T(8,128)(2,1)S(1)} all-gather(bf16[24,1536]{1,0:T(8,128)(2,1)S(1)} %copy_bitcast_fusion), channel_id=1, replica_groups=mesh['x_hi'=2,'y'=8,'x_lo'=2,'z_hi'=3,'z_lo'=4,'twin'=2] {'twin'}, dimensions={0}, use_global_device_ids=true | all-gather | bytes 221184 | tf_op jit(solution)/shard_map/all_gather | solution.py:26
  51.6 22.7 %all_gather.18 = bf16[288,1536]{1,0:T(8,128)(2,1)S(1)} all-gather(bf16[24,1536]{1,0:T(8,128)(2,1)S(1)} %slice_select_fusion.1), channel_id=1, replica_groups=mesh['x_hi'=2,'y'=8,'x_lo'=2,'z_hi'=3,'z_lo'=4,'twin'=2] {'z_hi','z_lo'}, dimensions={0}, use_global_device_ids=true | all-gather | bytes 958464 | tf_op jit(solution)/shard_map/all_gather | solution.py:169
  74.2 0.0 all-to-all-done.1
  74.2 0.6 fusion.4.corr_ref
  74.9 0.7 shard_map.29
  75.6 2.2 %collective-permute-start = (bf16[304,384]{1,0:T(8,128)(2,1)S(1)}, bf16[304,384]{1,0:T(8,128)(2,1)S(1)}, u32[]{:S(2)}, u32[]{:S(2)}) collective-permute-start(bf16[304,384]{1,0:T(8,128)(2,1)S(1)} %shard_map.29), channel_id=1, source_target_pairs={{0,24},{24,0},{1,25},{25,1},{2,26},{26,2},{3,27},{27,3},{4,28},{28... | collective-permute-start | bytes 700424 | tf_op jit(solution)/shard_map/ppermute | solution.py:176
  77.8 4.6 %collective-permute-done.taken_ref = bf16[304,384]{1,0:T(8,128)(2,1)S(1)} collective-permute-done((bf16[304,384]{1,0:T(8,128)(2,1)S(1)}, bf16[304,384]{1,0:T(8,128)(2,1)S(1)}, u32[]{:S(2)}, u32[]{:S(2)}) %collective-permute-start) | collective-permute-done | bytes 233504 | tf_op jit(solution)/shard_map/ppermute | solution.py:176
  82.4 1.5 %shard_map.30 = bf16[12,288,128]{2,1,0:T(8,128)(2,1)S(1)} custom-call(s32[3]{0:T(128)S(1)} %pad_add_fusion.place_ref, f32[288,384]{1,0:T(8,128)S(1)} %fusion.4.corr_ref, bf16[304,384]{1,0:T(8,128)(2,1)S(1)} %collective-permute-done.taken_ref, bf16[384,1536]{1,0:T(8,128)(2,1)S(1)} %bitcast.34), custom_call_target="tpu_custom_call" | custom-call | tf_op jit(solution)/shard_map/pallas_call | solution.py:136
  83.9 21.9 %all_to_all.21 = bf16[12,288,128]{2,1,0:T(8,128)(2,1)S(1)} all-to-all(bf16[12,288,128]{2,1,0:T(8,128)(2,1)S(1)} %shard_map.30), channel_id=1, replica_groups=mesh['x_hi'=2,'y'=8,'x_lo'=2,'z_hi'=3,'z_lo'=4,'twin'=2] {'z_lo'}, dimensions={0} | all-to-all | bytes 1769472 | tf_op jit(solution)/shard_map/all_to_all | solution.py:179
  105.8 0.2 reduce_sum.51
  105.9 12.2 %all_to_all.22 = bf16[3,288,128]{2,1,0:T(8,128)(2,1)S(1)} all-to-all(bf16[3,288,128]{2,1,0:T(8,128)(2,1)S(1)} %reduce_sum.51), channel_id=1, replica_groups=mesh['x_hi'=2,'y'=8,'x_lo'=2,'z_hi'=3,'z_lo'=4,'twin'=2] {'z_hi'}, dimensions={0} | all-to-all | bytes 442368 | tf_op jit(solution)/shard_map/all_to_all | solution.py:182
  118.2 6.9 %all_gather.19 = f32[288,128]{1,0:T(8,128)S(1)} all-gather(f32[144,128]{1,0:T(8,128)S(1)} %slice_select_fusion.3), channel_id=1, replica_groups=mesh['x_hi'=2,'y'=8,'x_lo'=2,'z_hi'=3,'z_lo'=4,'twin'=2] {'twin'}, dimensions={0}, use_global_device_ids=true | all-gather | bytes 221184 | tf_op jit(solution)/shard_map/all_gather | solution.py:26
  125.2 0.7 copy.9
  (9 shorter events, 0.1 us)
Async XLA Ops:
  36.6 37.6 %all-to-all-start.1 = ((bf16[16,24,1536]{2,1,0:T(8,128)(2,1)}), bf16[16,24,1536]{2,1,0:T(8,128)(2,1)S(1)}, u32[]{:S(2)}, u32[]{:S(2)}) async-start(bf16[16,24,1536]{2,1,0:T(8,128)(2,1)} %broadcast_in_dim.2), calls=%async_computation.1 | async-start | bytes 2359296 | tf_op jit(solution)/shard_map/all_to_all | solution.py:22
  75.6 6.8 %collective-permute-start = (bf16[304,384]{1,0:T(8,128)(2,1)S(1)}, bf16[304,384]{1,0:T(8,128)(2,1)S(1)}, u32[]{:S(2)}, u32[]{:S(2)}) collective-permute-start(bf16[304,384]{1,0:T(8,128)(2,1)S(1)} %shard_map.29), channel_id=1, source_target_pairs={{0,24},{24,0},{1,25},{25,1},{2,26},{26,2},{3,27},{27,3},{4,28},{28... | collective-permute-start | bytes 700424 | tf_op jit(solution)/shard_map/ppermute | solution.py:176
